TPU v7x, 256 devices: a whole 4x4x8 slice. The times are simulated.
256 devices in a mesh: vol: 4 (over y_hi, core), zs: 64 (over y_lo, x, z).
Axes of the slice: x: 4, y: 4 (y_hi: 2, y_lo: 2; y = y_hi * 2 + y_lo), z: 8, core: 2. Of those that a mesh axis runs over, the one named last changes fastest.
Arguments:
- volume: bfloat16 [64, 1024, 256], P('zs', 'vol'), may hold values from -6 to 6
- first_weight: bfloat16 [9, 12], replicated, may hold values from -3 to 3
- first_offset: float32 [12], replicated, may hold values from -2 to 2
- second_weight: bfloat16 [9, 12, 12], replicated, may hold values from -0.875 to 0.875
- second_offset: float32 [12], replicated, may hold values from -2 to 2
- reduce_conv_weight: bfloat16 [4, 12, 24], replicated, may hold values from -1.25 to 1.25
- reduce_conv_bias: float32 [24], replicated, may hold values from -2 to 2
- deep_weight: bfloat16 [27, 24, 24], replicated, may hold values from -0.3125 to 0.3125
- deep_offset: float32 [24], replicated, may hold values from -2 to 2
Outputs:
- affinity: bfloat16 [64, 24, 512, 128], P(None, None, ('vol', 'zs'))
All inputs are finite; a program needn't handle non-finite values.
Results may differ from a plain program's by a relative error of at most 0.0065.
Values may be sent and summed in bfloat16 or wider, within the bound.
A program may use at most 192 MiB of HBM per device.

v0:
```python
import jax
import jax.numpy as jnp
from jax import lax
from jax.sharding import PartitionSpec as P


def extended(value, sides, width):
    for axis, dim in sides:
        size, length = (lax.axis_size(axis), value.shape[dim])
        up = [(i, (i + 1) % size) for i in range(size - 1)]
        down = [(j, i) for i, j in up]
        last = lax.slice_in_dim(value, length - width, length, axis=dim)
        first = lax.slice_in_dim(value, 0, width, axis=dim)
        before = lax.ppermute(last, axis, up)
        after = lax.ppermute(first, axis, down)
        value = jnp.concatenate([before, value, after], axis=dim)
    return value


def plane_conv(field, weight, offset):
    padded = jnp.pad(field, ((0, 0), (0, 0), (0, 0), (1, 1)))
    row_count = field.shape[2] - 2
    col_count = field.shape[3]
    summed = jnp.zeros((field.shape[0], weight.shape[2], row_count, col_count), jnp.float32)
    for along_x in range(3):
        for along_y in range(3):
            window = padded[:, :, along_x : along_x + row_count, along_y : along_y + col_count]
            summed = summed + jnp.einsum(
                "zcxy,cd->zdxy",
                window,
                weight[3 * along_x + along_y],
                preferred_element_type=jnp.float32,
            )
    return summed + offset[None, :, None, None]


def leading_section(
    rimmed, at_top, at_bottom, first_weight, first_offset, second_weight, second_offset, rim_rows
):
    field = rimmed[:, None]
    first = jax.nn.relu(plane_conv(field, first_weight[:, None, :], first_offset))
    row_ids = lax.broadcasted_iota(jnp.int32, first.shape, 2)
    last_row = first.shape[2] - 1
    outside = (row_ids < rim_rows - 1) & at_top | (row_ids > last_row - (rim_rows - 1)) & at_bottom
    first = jnp.where(outside, 0.0, first).astype(jnp.bfloat16)
    return jax.nn.relu(plane_conv(first, second_weight, second_offset)).astype(jnp.bfloat16)


def halve_resolution(latter_conv, reduce_conv_weight, reduce_conv_bias):
    depth, channels, fine_rows, fine_cols = latter_conv.shape
    blocks = latter_conv.reshape(depth, channels, fine_rows // 2, 2, fine_cols // 2, 2)
    kernel = reduce_conv_weight.reshape(2, 2, channels, reduce_conv_weight.shape[2])
    summed = jnp.einsum("zcxayb,abcd->zdxy", blocks, kernel, preferred_element_type=jnp.float32)
    return jax.nn.relu(summed + reduce_conv_bias[None, :, None, None]).astype(jnp.bfloat16)


def reduced_row_span(coarse):
    return extended(coarse, ((("vol", "zs"), 2),), 1)


def deep_conv(rimmed, deep_weight, deep_offset):
    padded = jnp.pad(rimmed, ((1, 1), (0, 0), (0, 0), (1, 1)))
    depth = rimmed.shape[0]
    row_count = rimmed.shape[2] - 2
    col_count = rimmed.shape[3]
    summed = jnp.zeros((depth, deep_weight.shape[2], row_count, col_count), jnp.float32)
    for along_z in range(3):
        for along_x in range(3):
            for along_y in range(3):
                window = padded[
                    along_z : along_z + depth,
                    :,
                    along_x : along_x + row_count,
                    along_y : along_y + col_count,
                ]
                summed = summed + jnp.einsum(
                    "zcxy,cd->zdxy",
                    window,
                    deep_weight[9 * along_z + 3 * along_x + along_y],
                    preferred_element_type=jnp.float32,
                )
    return jax.nn.relu(summed + deep_offset[None, :, None, None]).astype(jnp.bfloat16)


def shards(
    volume,
    first_weight,
    first_offset,
    second_weight,
    second_offset,
    reduce_conv_weight,
    reduce_conv_bias,
    deep_weight,
    deep_offset,
):
    rimmed = extended(volume, (("vol", 1),), 2)
    position = lax.axis_index("vol")
    members = lax.axis_size("vol")
    latter_conv = leading_section(
        rimmed,
        position == 0,
        position == members - 1,
        first_weight,
        first_offset,
        second_weight,
        second_offset,
        2,
    )
    resident_reduced = halve_resolution(latter_conv, reduce_conv_weight, reduce_conv_bias)
    coarse = lax.all_to_all(resident_reduced, "zs", split_axis=2, concat_axis=0, tiled=True)
    return deep_conv(reduced_row_span(coarse), deep_weight, deep_offset)


def solution(mesh):
    return jax.shard_map(
        shards,
        mesh=mesh,
        in_specs=(P("zs", "vol", None), P(), P(), P(), P(), P(), P(), P(), P()),
        out_specs=P(None, None, ("vol", "zs"), None),
        check_vma=False,
    )
```

profile of v0, /device:TPU:1, one launch (start us, length us, event | category | flops | bytes accessed | tf_op | source)
XLA Modules:
  0.0 200.4 jit_solution(12836554589089434173)
XLA Ops:
  0.7 6.2 %collective-permute-start = (bf16[1,2,256]{2,1,0:T(2,128)(2,1)S(1)}, bf16[1,2,256]{2,1,0:T(2,128)(2,1)S(1)}, u32[]{:S(2)}, u32[]{:S(2)}) collective-permute-start(bf16[1,2,256]{2,1,0:T(2,128)(2,1)S(1)} %get-tuple-element.43), channel_id=1, source_target_pairs={{0,64},{64,128},{128,192},{1,65},{65,129},{129,193},{2,66},{66,130... | collective-permute-start | bytes 3080 | tf_op jit(solution)/shard_map/ppermute | solution.py:14
  6.9 1.9 collective-permute-start.1
  9.9 3.4 %collective-permute-done.1 = bf16[1,2,256]{2,1,0:T(2,128)(2,1)S(1)} collective-permute-done((bf16[1,2,256]{2,1,0:T(2,128)(2,1)S(1)}, bf16[1,2,256]{2,1,0:T(2,128)(2,1)S(1)}, u32[]{:S(2)}, u32[]{:S(2)}) %collective-permute-start.1) | collective-permute-done | bytes 1056 | tf_op jit(solution)/shard_map/ppermute | solution.py:15
  14.6 9.0 %fusion.8 = bf16[1,12,258,256]{3,1,2,0:T(8,128)(2,1)S(1)} fusion(f32[12]{0:T(128)S(1)} %copy-done.9, f32[12]{0:T(128)S(1)} %get-tuple-element.52, f32[258,256]{1,0:T(8,128)S(1)} %get-tuple-element.39, f32[12]{0:T(128)S(1)} %get-tuple-element.53, f32[258,256]{1,0:T(8,128)S(1)} %get-tuple-element.40, f32[12]{0:T(128)S(1)} %get-tuple-element.46, ...), kind=kLoop, calls=%fused_computation.22 | loop fusion | flops 16644096 | bytes 3963618 | tf_op jit(solution)/shard_map/convert_element_type | solution.py:45
  25.4 2.8 %fusion.19 = f32[256,256,12]{1,2,0:T(8,128)} fusion(bf16[1,12,258,256]{3,1,2,0:T(8,128)(2,1)S(1)} %fusion.8, bf16[9,12,12]{2,1,0:T(8,128)(2,1)S(1)} %copy-done.1), kind=kOutput, calls=%fused_computation.30 | convolution fusion | flops 18874368 | bytes 5263360 | tf_op jit(solution)/shard_map/zcxy,cd->zdxy/dot_general | solution.py:28
  28.2 2.9 %fusion.22 = f32[256,256,12]{1,2,0:T(8,128)} fusion(bf16[1,12,258,256]{3,1,2,0:T(8,128)(2,1)S(1)} %fusion.8, bf16[9,12,12]{2,1,0:T(8,128)(2,1)S(1)} %copy-done.1), kind=kOutput, calls=%fused_computation.32 | convolution fusion | flops 18874368 | bytes 5263360 | tf_op jit(solution)/shard_map/zcxy,cd->zdxy/dot_general | solution.py:28
  31.1 2.7 %fusion.26 = f32[256,256,12]{1,2,0:T(8,128)} fusion(bf16[1,12,258,256]{3,1,2,0:T(8,128)(2,1)S(1)} %fusion.8, bf16[9,12,12]{2,1,0:T(8,128)(2,1)S(1)} %copy-done.1), kind=kOutput, calls=%fused_computation.35 | convolution fusion | flops 18874368 | bytes 5246976 | tf_op jit(solution)/shard_map/zcxy,cd->zdxy/dot_general | solution.py:28
  33.8 2.7 %fusion.27 = f32[256,256,12]{1,2,0:T(8,128)} fusion(bf16[1,12,258,256]{3,1,2,0:T(8,128)(2,1)S(1)} %fusion.8, bf16[9,12,12]{2,1,0:T(8,128)(2,1)S(1)} %copy-done.1), kind=kOutput, calls=%fused_computation.37 | convolution fusion | flops 18874368 | bytes 5246976 | tf_op jit(solution)/shard_map/zcxy,cd->zdxy/dot_general | solution.py:28
  36.5 2.8 %fusion.28 = f32[256,256,12]{1,2,0:T(8,128)} fusion(bf16[1,12,258,256]{3,1,2,0:T(8,128)(2,1)S(1)} %fusion.8, bf16[9,12,12]{2,1,0:T(8,128)(2,1)S(1)} %copy-done.1), kind=kOutput, calls=%fused_computation.39 | convolution fusion | flops 18874368 | bytes 5246976 | tf_op jit(solution)/shard_map/zcxy,cd->zdxy/dot_general | solution.py:28
  39.2 2.8 %fusion.10 = f32[256,256,12]{1,2,0:T(8,128)} fusion(bf16[1,12,258,256]{3,1,2,0:T(8,128)(2,1)S(1)} %fusion.8, bf16[9,12,12]{2,1,0:T(8,128)(2,1)S(1)} %copy-done.1), kind=kOutput, calls=%fused_computation.24 | convolution fusion | flops 18874368 | bytes 5263360 | tf_op jit(solution)/shard_map/zcxy,cd->zdxy/dot_general | solution.py:28
  42.0 11.1 %fusion.29 = bf16[12,256,256]{2,0,1:T(8,128)(2,1)} fusion(f32[12]{0:T(128)S(1)} %copy-done.10, bf16[1,12,258,256]{3,1,2,0:T(8,128)(2,1)S(1)} %fusion.8, f32[256,256,12]{1,2,0:T(8,128)} %fusion.26, f32[256,256,12]{1,2,0:T(8,128)} %fusion.22, f32[256,256,12]{1,2,0:T(8,128)} %fusion.19, f32[256,256,12]{1,2,0:T(8,128)} %fusion.27, ...), kind=kOutput, calls=%fused_computation.40 | convolution fusion | flops 27525120 | bytes 30953984 | tf_op jit(solution)/shard_map/zcxy,cd->zdxy/dot_general | solution.py:28
  53.1 12.8 %copy.98 = bf16[12,256,256]{0,2,1:T(8,128)(2,1)} copy(bf16[12,256,256]{2,0,1:T(8,128)(2,1)} %fusion.29) | data formatting | bytes 3145728 | tf_op jit(solution)/shard_map/convert_element_type | solution.py:46
  65.9 9.3 %fusion.39 = bf16[1,24,128,128]{3,1,0,2:T(8,128)(2,1)} fusion(bf16[12,128,2,128,2]{0,4,3,2,1:T(2,128)(2,1)} %bitcast.421, f32[24]{0:T(128)S(1)} %copy-done.13, bf16[2,2,12,24]{3,1,0,2:T(2,128)(2,1)S(1)} %bitcast.422), kind=kOutput, calls=%fused_computation.57 | convolution fusion | flops 38928384 | bytes 2361696 | tf_op jit(solution)/shard_map/zcxayb,abcd->zdxy/dot_general | solution.py:53
  75.2 11.9 %all-to-all-start = ((bf16[1,24,128,128]{3,1,0,2:T(8,128)(2,1)}), bf16[1,24,128,128]{3,1,0,2:T(8,128)(2,1)S(1)}, u32[]{:S(2)}, u32[]{:S(2)}) async-start(bf16[1,24,128,128]{3,1,0,2:T(8,128)(2,1)} %fusion.39), calls=%async_computation | async-start | bytes 1572864 | tf_op jit(solution)/shard_map/all_to_all | solution.py:110
  87.2 1.8 fusion.172
  89.0 20.0 %all-to-all-done = bf16[1,24,128,128]{3,1,0,2:T(8,128)(2,1)S(1)} async-done(((bf16[1,24,128,128]{3,1,0,2:T(8,128)(2,1)}), bf16[1,24,128,128]{3,1,0,2:T(8,128)(2,1)S(1)}, u32[]{:S(2)}, u32[]{:S(2)}) %all-to-all-start) | async-done | bytes 786464 | tf_op jit(solution)/shard_map/all_to_all | solution.py:110
  109.9 2.9 %collective-permute-start.2 = (bf16[64,24,1,128]{3,1,2,0:T(8,128)(2,1)}, bf16[64,24,1,128]{3,1,2,0:T(8,128)(2,1)S(1)}, u32[]{:S(2)}, u32[]{:S(2)}) collective-permute-start(bf16[64,24,1,128]{3,1,2,0:T(8,128)(2,1)} %get-tuple-element.5), channel_id=1, source_target_pairs={{0,1},{1,2},{2,3},{3,4},{4,5},{5,6},{6,7},{7,8},{8,9},{9,10},{10,1... | collective-permute-start | bytes 1179656 | tf_op jit(solution)/shard_map/ppermute | solution.py:14
  112.9 6.8 %collective-permute-start.3 = (bf16[64,24,1,128]{3,1,2,0:T(8,128)(2,1)}, bf16[64,24,1,128]{3,1,2,0:T(8,128)(2,1)S(1)}, u32[]{:S(2)}, u32[]{:S(2)}) collective-permute-start(bf16[64,24,1,128]{3,1,2,0:T(8,128)(2,1)} %get-tuple-element.6), channel_id=1, source_target_pairs={{1,0},{2,1},{3,2},{4,3},{5,4},{6,5},{7,6},{8,7},{9,8},{10,9},{11,1... | collective-permute-start | bytes 1179656 | tf_op jit(solution)/shard_map/ppermute | solution.py:15
  132.5 1.7 copy.191
  134.2 1.7 copy.190
  135.9 1.7 copy.189
  137.6 1.7 copy.188
  146.5 4.1 %select_maximum_fusion = bf16[66,24,4,130]{3,1,2,0:T(8,128)(2,1)S(1)} fusion(bf16[64,24,1,128]{3,1,2,0:T(8,128)(2,1)S(1)} %collective-permute-done.3, bf16[64,24,2,128]{3,1,2,0:T(8,128)(2,1)S(1)} %bitcast.418, bf16[64,24,1,128]{3,1,2,0:T(8,128)(2,1)S(1)} %collective-permute-done.2), kind=kLoop, calls=%fused_computation.17 | loop fusion | flops 15649920 | bytes 3220224 | tf_op jit(solution)/shard_map/concatenate | solution.py:16
  186.6 12.3 %fusion.36 = bf16[64,24,2,128]{3,1,2,0:T(8,128)(2,1)S(1)} fusion(f32[64,2,128,24]{2,3,1,0:T(8,128)S(1)} %fusion.51, f32[64,2,128,24]{2,3,1,0:T(8,128)} %fusion.53, f32[64,2,128,24]{2,3,1,0:T(8,128)} %fusion.55, f32[64,2,128,24]{2,3,1,0:T(8,128)} %fusion.57, f32[64,2,128,24]{2,3,1,0:T(8,128)} %fusion.59, f32[64,2,128,24]{2,3,1,0:T(8,128)} %fusion.61, ...), kind=kOutput, calls=%fused_computation.47 | convolution fusion | flops 30277632 | bytes 42473984 | tf_op jit(solution)/shard_map/zcxy,cd->zdxy/dot_general | solution.py:76
  (90 shorter events, 62.9 us)
Async XLA Ops:
  0.0 14.6 %copy-start.9 = (f32[12]{0:T(128)S(1)}, f32[12]{0:T(128)}, u32[]{:S(2)}) copy-start(f32[12]{0:T(128)} %param.11) | copy-start | bytes 148
  0.7 9.1 %collective-permute-start = (bf16[1,2,256]{2,1,0:T(2,128)(2,1)S(1)}, bf16[1,2,256]{2,1,0:T(2,128)(2,1)S(1)}, u32[]{:S(2)}, u32[]{:S(2)}) collective-permute-start(bf16[1,2,256]{2,1,0:T(2,128)(2,1)S(1)} %get-tuple-element.43), channel_id=1, source_target_pairs={{0,64},{64,128},{128,192},{1,65},{65,129},{129,193},{2,66},{66,130... | collective-permute-start | bytes 3080 | tf_op jit(solution)/shard_map/ppermute | solution.py:14
  6.9 6.4 %collective-permute-start.1 = (bf16[1,2,256]{2,1,0:T(2,128)(2,1)S(1)}, bf16[1,2,256]{2,1,0:T(2,128)(2,1)S(1)}, u32[]{:S(2)}, u32[]{:S(2)}) collective-permute-start(bf16[1,2,256]{2,1,0:T(2,128)(2,1)S(1)} %get-tuple-element.44), channel_id=1, source_target_pairs={{64,0},{128,64},{192,128},{65,1},{129,65},{193,129},{66,2},{130,66... | collective-permute-start | bytes 3080 | tf_op jit(solution)/shard_map/ppermute | solution.py:15
  14.6 9.0 %copy-start.1 = (bf16[9,12,12]{2,1,0:T(8,128)(2,1)S(1)}, bf16[9,12,12]{2,1,0:T(8,128)(2,1)}, u32[]{:S(2)}) copy-start(bf16[9,12,12]{2,1,0:T(8,128)(2,1)} %param.12) | copy-start | bytes 7780
  39.2 2.8 %copy-start.10 = (f32[12]{0:T(128)S(1)}, f32[12]{0:T(128)}, u32[]{:S(2)}) copy-start(f32[12]{0:T(128)} %param.13) | copy-start | bytes 148
  53.1 12.8 %copy-start.12 = (bf16[4,12,24]{2,0,1:T(4,128)(2,1)S(1)}, bf16[4,12,24]{2,0,1:T(4,128)(2,1)}, u32[]{:S(2)}) copy-start(bf16[4,12,24]{2,0,1:T(4,128)(2,1)} %param.14) | copy-start | bytes 6916
  53.1 12.8 %copy-start.13 = (f32[24]{0:T(128)S(1)}, f32[24]{0:T(128)}, u32[]{:S(2)}) copy-start(f32[24]{0:T(128)} %param.15) | copy-start | bytes 292
  75.2 11.9 %copy-start = (bf16[27,24,24]{0,2,1:T(8,128)(2,1)S(1)}, bf16[27,24,24]{0,2,1:T(8,128)(2,1)}, u32[]{:S(2)}) copy-start(bf16[27,24,24]{0,2,1:T(8,128)(2,1)} %param.16) | copy-start | bytes 93316
  75.2 33.8 %all-to-all-start = ((bf16[1,24,128,128]{3,1,0,2:T(8,128)(2,1)}), bf16[1,24,128,128]{3,1,0,2:T(8,128)(2,1)S(1)}, u32[]{:S(2)}, u32[]{:S(2)}) async-start(bf16[1,24,128,128]{3,1,0,2:T(8,128)(2,1)} %fusion.39), calls=%async_computation | async-start | bytes 1572864 | tf_op jit(solution)/shard_map/all_to_all | solution.py:110
  109.9 36.5 %collective-permute-start.2 = (bf16[64,24,1,128]{3,1,2,0:T(8,128)(2,1)}, bf16[64,24,1,128]{3,1,2,0:T(8,128)(2,1)S(1)}, u32[]{:S(2)}, u32[]{:S(2)}) collective-permute-start(bf16[64,24,1,128]{3,1,2,0:T(8,128)(2,1)} %get-tuple-element.5), channel_id=1, source_target_pairs={{0,1},{1,2},{2,3},{3,4},{4,5},{5,6},{6,7},{7,8},{8,9},{9,10},{10,1... | collective-permute-start | bytes 1179656 | tf_op jit(solution)/shard_map/ppermute | solution.py:14
  112.9 33.6 %collective-permute-start.3 = (bf16[64,24,1,128]{3,1,2,0:T(8,128)(2,1)}, bf16[64,24,1,128]{3,1,2,0:T(8,128)(2,1)S(1)}, u32[]{:S(2)}, u32[]{:S(2)}) collective-permute-start(bf16[64,24,1,128]{3,1,2,0:T(8,128)(2,1)} %get-tuple-element.6), channel_id=1, source_target_pairs={{1,0},{2,1},{3,2},{4,3},{5,4},{6,5},{7,6},{8,7},{9,8},{10,9},{11,1... | collective-permute-start | bytes 1179656 | tf_op jit(solution)/shard_map/ppermute | solution.py:15
  150.6 0.7 copy-start.2
  150.7 2.2 %copy-start.3 = (bf16[1,24,24]{1,2,0:T(8,128)(2,1)S(1)}, bf16[1,24,24]{1,2,0:T(8,128)(2,1)}, u32[]{:S(2)}) copy-start(bf16[1,24,24]{1,2,0:T(8,128)(2,1)} %copy.190) | copy-start | bytes 3460
  151.3 3.1 %copy-start.4 = (bf16[1,24,24]{1,2,0:T(8,128)(2,1)S(1)}, bf16[1,24,24]{1,2,0:T(8,128)(2,1)}, u32[]{:S(2)}) copy-start(bf16[1,24,24]{1,2,0:T(8,128)(2,1)} %copy.189) | copy-start | bytes 3460
  152.9 3.2 %copy-start.5 = (bf16[1,24,24]{1,2,0:T(8,128)(2,1)S(1)}, bf16[1,24,24]{1,2,0:T(8,128)(2,1)}, u32[]{:S(2)}) copy-start(bf16[1,24,24]{1,2,0:T(8,128)(2,1)} %copy.188) | copy-start | bytes 3460
  154.4 3.1 %copy-start.6 = (bf16[1,24,24]{1,2,0:T(8,128)(2,1)S(1)}, bf16[1,24,24]{1,2,0:T(8,128)(2,1)}, u32[]{:S(2)}) copy-start(bf16[1,24,24]{1,2,0:T(8,128)(2,1)} %copy.187) | copy-start | bytes 3460
  156.0 3.1 %copy-start.7 = (bf16[1,24,24]{1,2,0:T(8,128)(2,1)S(1)}, bf16[1,24,24]{1,2,0:T(8,128)(2,1)}, u32[]{:S(2)}) copy-start(bf16[1,24,24]{1,2,0:T(8,128)(2,1)} %copy.186) | copy-start | bytes 3460
  157.6 3.3 %copy-start.8 = (bf16[1,24,24]{1,2,0:T(8,128)(2,1)S(1)}, bf16[1,24,24]{1,2,0:T(8,128)(2,1)}, u32[]{:S(2)}) copy-start(bf16[1,24,24]{1,2,0:T(8,128)(2,1)} %copy.185) | copy-start | bytes 3460
  185.9 0.7 copy-start.11
where the time goes:
time: 201 us; the launch traced here: 200 us
  matrix products  87 us (43%)
  local copies, waits for them, and re-layouts  44.5 us (22%)
  starting transfers between devices  29.8 us (15%)
  waiting for transfers between devices  23.5 us (12%)
  other arithmetic  15.4 us (8%)
    dot_general x27, matrix products, deep_conv(): jnp.einsum('zcxy,cd->zdxy', window, deep_weight[9 * along_z + 3 * along_x...  48.3 us
    dot_general x9, matrix products, plane_conv(): jnp.einsum('zcxy,cd->zdxy', window, weight[3 * along_x + along_y], prefer...  29.4 us
    unnamed x55, local copies, waits for them, and re-layouts  25.3 us
    all_to_all x1, waiting for transfers between devices, shards(): lax.all_to_all(resident_reduced, 'zs', split_axis=2, concat_axis=0, tiled...  20 us
    convert_element_type x1, local copies, waits for them, and re-layouts, leading_section(): jax.nn.relu(plane_conv(first, second_weight, second_offset))  12.8 us
    all_to_all x1, starting transfers between devices, shards(): lax.all_to_all(resident_reduced, 'zs', split_axis=2, concat_axis=0, tiled...  11.9 us
    dot_general x1, matrix products, halve_resolution(): jnp.einsum('zcxayb,abcd->zdxy', blocks, kernel, preferred_element_type=jn...  9.33 us
    ppermute x2, starting transfers between devices, extended(): before = lax.ppermute(last, axis, up)  9.13 us
  transfers between devices with their start and end apart: 5, of which 2 were waited for; matrix products, arithmetic and copies ran while one was open for 15% of the time, Pallas kernels for 0%

commit v1 on v0

v1 whole, which is shorter than its diff:
```python
import functools

import jax
import jax.numpy as jnp
import numpy as np
from jax import lax
from jax.experimental import pallas as pl
from jax.experimental.pallas import tpu as pltpu
from jax.sharding import PartitionSpec as P

BF16 = jnp.bfloat16
F32 = jnp.float32
MESH = pl.DeviceIdType.MESH
DEPTH = 64
HALF = DEPTH // 2


def tables():
    place1 = np.zeros((3, 256, 12), np.float32)
    mask1 = np.zeros((256, 180), np.float32)
    pick1 = np.zeros((180, 9), np.float32)
    lay1 = np.zeros((180, 72), np.float32)
    source = ({0: (0, 1), 1: (1, 0), 2: (1, 1)}, {0: (1, 0), 1: (1, 1), 2: (2, 0)})
    for parity in range(2):
        for row in range(10):
            kind = parity * 10 + row
            for chan in range(12):
                at = parity * 128 + chan * 10 + row
                place1[0, at, chan] = 1
                place1[1, at, chan] = row >= 3
                place1[2, at, chan] = row < 7
                mask1[at, kind * 9 : kind * 9 + 9] = 1
            for along_x in range(3):
                for along_y in range(3):
                    tap = 3 * along_x + along_y
                    pick1[kind * 9 + tap, tap] = 1
                    shift, origin = source[parity][along_y]
                    fine = row + along_x
                    column = shift * 24 + (fine // 4) * 8 + origin * 4 + fine % 4
                    lay1[kind * 9 + tap, column] = 1
    place2 = np.zeros((96, 12), np.float32)
    lay2 = np.zeros((9, 12, 1024), np.float32)
    block = ({0: 0, 1: 1, 2: 2}, {0: 1, 1: 2, 2: 3})
    for chan in range(12):
        place2[chan * 8 : chan * 8 + 8, chan] = 1
        for along_x in range(3):
            for along_y in range(3):
                for parity in range(2):
                    column = parity * 512 + block[parity][along_y] * 128 + chan * 10 + along_x
                    lay2[3 * along_x + along_y, chan, column] = 1
    place3 = np.zeros((3, 96, 24), np.float32)
    for chan in range(24):
        for row in range(4):
            place3[0, chan * 4 + row, chan] = 1
            place3[1, chan * 4 + row, chan] = row >= 1
            place3[2, chan * 4 + row, chan] = row < 3
    lay3 = np.zeros((4, 12, 256), np.float32)
    for a in range(2):
        for b in range(2):
            for chan in range(12):
                lay3[2 * a + b, chan, b * 96 + chan * 8 + a] = 1
    place4 = np.zeros((48, 24), np.float32)
    lay4 = np.zeros((216, 384), np.float32)
    for chan in range(24):
        place4[chan * 2 : chan * 2 + 2, chan] = 1
        for along_x in range(3):
            for along_y in range(3):
                lay4[along_x * 72 + along_y * 24 + chan, along_y * 96 + chan * 4 + along_x] = 1
    made = (place1, mask1, pick1, lay1, place2, lay2, place3, lay3, place4, lay4)
    return [table.astype(jnp.bfloat16) for table in made]


def mul(a, b):
    return jnp.dot(a, b, preferred_element_type=F32)


def mul_t(a, b):
    return lax.dot_general(a, b, (((1,), (1,)), ((), ())), preferred_element_type=F32)


def column(place, offset):
    summed = jnp.sum(place.astype(F32) * offset, axis=1, keepdims=True)
    return jnp.broadcast_to(summed, (place.shape[0], 128))


def lay_weights(edge, raw, consts, laid):
    w1_ref, o1_ref, w2_ref, o2_ref, w3_ref, o3_ref, w4_ref, o4_ref = raw
    place1, mask1, pick1, lay1, place2, lay2, place3, lay3, place4, lay4 = consts
    m1, b1, m2, b2, m3, b3, m4, b4 = laid

    here1 = place1[edge]
    taps = mul(pick1[...], w1_ref[...]).astype(BF16)
    chosen = mul_t(here1, taps) * mask1[...].astype(F32)
    m1[...] = mul(chosen.astype(BF16), lay1[...]).astype(BF16)
    b1[...] = column(here1, o1_ref[...])

    here2 = place2[...]
    base = jnp.zeros((96, 1024), F32)
    for tap in range(9):
        base = base + mul(mul_t(here2, w2_ref[tap]).astype(BF16), lay2[tap])
    for parity in range(2):
        for block in range(4):
            start = parity * 512 + block * 128
            rows = [
                pltpu.roll(base[8 * c : 8 * c + 8, start : start + 128], 0, 1, stride=1, stride_axis=0)
                for c in range(12)
            ]
            m2[96 * parity : 96 * parity + 96, 128 * block : 128 * block + 128] = jnp.concatenate(
                rows, axis=0
            ).astype(BF16)
    offset2 = column(here2, o2_ref[...])
    b2[:96] = offset2
    b2[96:] = offset2

    here3 = place3[edge]
    base = jnp.zeros((96, 256), F32)
    for tap in range(4):
        base = base + mul(mul_t(here3, w3_ref[tap]).astype(BF16), lay3[tap])
    row = lax.broadcasted_iota(jnp.int32, base.shape, 0) & 3
    placed = base
    for r in range(1, 4):
        placed = jnp.where(row == r, pltpu.roll(base, 2 * r, 1), placed)
    m3[...] = placed[:, :192].astype(BF16)
    b3[...] = column(here3, o3_ref[...])

    here4 = place4[...]
    for dz in range(3):
        base = mul(mul_t(here4, w4_ref[dz]).astype(BF16), lay4[...])
        row = lax.broadcasted_iota(jnp.int32, base.shape, 0) & 1
        placed = jnp.where(row == 1, pltpu.roll(base, 1, 1), base)
        m4[48 * dz : 48 * dz + 48] = placed[:, :288].astype(BF16)
    b4[...] = column(here4, o4_ref[...])


def from_left(value, lane):
    return jnp.where(lane == 0, 0.0, pltpu.roll(value, 1, 1))


def from_right(value, lane):
    return jnp.where(lane == 127, 0.0, pltpu.roll(value, 127, 1))


def both(function, value):
    lane = lax.broadcasted_iota(jnp.int32, (value.shape[0], 128), 1)
    return jnp.concatenate([function(value[:, :128], lane), function(value[:, 128:], lane)], axis=1)


def twice(bias):
    return jnp.concatenate([bias, bias], axis=1)


def relu(value):
    return jnp.maximum(value, 0.0)


def coarse_of(field, laid):
    m1, b1, m2, b2, m3, b3, _, _ = laid
    stacked = jnp.concatenate([both(from_left, field), field, both(from_right, field)], axis=0)
    first = relu(mul(m1[...], stacked.astype(BF16)) + twice(b1[...]))
    even, odd = first[:128], first[128:]
    stacked = jnp.concatenate([both(from_left, odd), even, odd, both(from_right, even)], axis=0)
    second = relu(mul(m2[...], stacked.astype(BF16)) + twice(b2[...])).astype(BF16)
    return relu(mul(m3[...], second) + twice(b3[...]))


def conv_kernel(*refs):
    x_ref, raw, consts, out_ref = refs[0], refs[1:9], refs[9:19], refs[19]
    laid = refs[20:28]
    ahead_ref, lower_ref = refs[28:30]
    position = lax.axis_index("vol") * lax.axis_size("zs") + lax.axis_index("zs")
    last = lax.axis_size("vol") * lax.axis_size("zs") - 1
    edge = jnp.where(position == 0, 1, jnp.where(position == last, 2, 0))
    lay_weights(edge, raw, consts, laid)
    m4, b4 = laid[6:8]

    def step(pair, carry):
        closing, opening = carry
        low = x_ref[pair].astype(F32).reshape(24, 128)
        high = x_ref[pair + HALF].astype(F32).reshape(24, 128)
        coarse = coarse_of(jnp.concatenate([low, high], axis=1), laid)
        stacked = jnp.concatenate([both(from_left, coarse), coarse, both(from_right, coarse)], axis=0)
        deep = mul(m4[...], stacked.astype(BF16))
        total = closing + deep[96:]
        ahead_ref[pair] = deep[96:, 128:]
        lower_ref[pair] = total[:, 128:]
        done = relu(total + twice(b4[...])).astype(BF16)
        slot = jnp.maximum(pair - 1, 0)
        out_ref[slot] = done[:, :128]
        out_ref[slot + HALF] = done[:, 128:]
        return opening + deep[48:96], deep[:48]

    zero = jnp.zeros((48, 256), F32)
    closing, opening = lax.fori_loop(0, HALF, step, (zero, zero), unroll=2)
    bias = b4[...]
    out_ref[HALF - 1] = relu(closing[:, :128] + ahead_ref[0] + bias).astype(BF16)
    out_ref[DEPTH - 1] = relu(closing[:, 128:] + bias).astype(BF16)
    out_ref[HALF] = relu(lower_ref[1] + opening[:, :128] + bias).astype(BF16)


def exchange_kernel(volume_ref, got_ref, tiles, halo_send, halo_recv, send_sem, recv_sem):
    vol, me = lax.axis_index("vol"), lax.axis_index("zs")
    vols, members = lax.axis_size("vol"), lax.axis_size("zs")

    barrier = pltpu.get_barrier_semaphore()

    def greet(step, carry):
        pl.semaphore_signal(
            barrier, inc=1, device_id=(vol, lax.rem(me + step, members)), device_id_type=MESH
        )
        return carry

    @pl.when(vol > 0)
    def _():
        pl.semaphore_signal(barrier, inc=1, device_id=(vol - 1, me), device_id_type=MESH)

    @pl.when(vol < vols - 1)
    def _():
        pl.semaphore_signal(barrier, inc=1, device_id=(vol + 1, me), device_id_type=MESH)

    lax.fori_loop(1, members, greet, 0)

    line = lax.broadcasted_iota(jnp.int32, (256, 256), 0)
    lane = lax.broadcasted_iota(jnp.int32, (256, 256), 1)
    parted = (line == jnp.where(lane < 128, 2 * lane, 2 * lane - 255)).astype(F32).astype(BF16)
    split = mul(volume_ref[0], parted)
    even = split[:, :128].reshape(32, 8, 128)
    odd = split[:, 128:].reshape(32, 8, 128)
    row = lax.broadcasted_iota(jnp.int32, (32, 8, 128), 1)
    upper = jnp.where(row < 4, even, pltpu.roll(odd, 4, 1))
    lower = jnp.where(row < 4, pltpu.roll(even, 4, 1), odd)
    tiles[1:65] = jnp.stack([upper, lower], axis=1).reshape(64, 8, 128).astype(BF16)

    @pl.when(vol == 0)
    def _():
        tiles[0] = jnp.zeros((8, 128), BF16)

    @pl.when(vol == vols - 1)
    def _():
        tiles[65] = jnp.zeros((8, 128), BF16)

    pl.semaphore_wait(
        barrier, members - 1 + jnp.where(vol > 0, 1, 0) + jnp.where(vol < vols - 1, 1, 0)
    )

    def upward():
        return pltpu.make_async_remote_copy(
            src_ref=tiles.at[1],
            dst_ref=tiles.at[65],
            send_sem=halo_send.at[0],
            recv_sem=halo_recv.at[0],
            device_id=(vol - 1, me),
            device_id_type=MESH,
        )

    def downward():
        return pltpu.make_async_remote_copy(
            src_ref=tiles.at[64],
            dst_ref=tiles.at[0],
            send_sem=halo_send.at[1],
            recv_sem=halo_recv.at[1],
            device_id=(vol + 1, me),
            device_id_type=MESH,
        )

    @pl.when(vol > 0)
    def _():
        upward().start()

    @pl.when(vol < vols - 1)
    def _():
        downward().start()

    def give(target):
        pltpu.make_async_remote_copy(
            src_ref=tiles.at[pl.ds(target, 3)],
            dst_ref=got_ref.at[me],
            send_sem=send_sem,
            recv_sem=recv_sem,
            device_id=(vol, target),
            device_id_type=MESH,
        ).start()

    def send(step, carry):
        target = lax.rem(me + step, members)

        @pl.when((target != 0) & (target != members - 1))
        def _():
            give(target)

        return carry

    lax.fori_loop(1, members, send, 0)

    @pl.when(vol < vols - 1)
    def _():
        upward().wait_recv()

    @pl.when(vol > 0)
    def _():
        downward().wait_recv()

    @pl.when(me != 0)
    def _():
        give(0)

    @pl.when(me != members - 1)
    def _():
        give(members - 1)

    got_ref[me] = tiles[pl.ds(me, 3)]

    @pl.when(vol > 0)
    def _():
        upward().wait_send()

    @pl.when(vol < vols - 1)
    def _():
        downward().wait_send()

    rest = got_ref.at[pl.ds(0, 63)]
    pltpu.make_async_copy(rest, rest, send_sem).wait()
    pltpu.make_async_copy(rest, rest, recv_sem).wait()


VMEM = pl.BlockSpec(memory_space=pltpu.VMEM)


def exchange(volume):
    return pl.pallas_call(
        exchange_kernel,
        out_shape=jax.ShapeDtypeStruct((DEPTH, 3, 8, 128), BF16),
        in_specs=[VMEM],
        out_specs=VMEM,
        scratch_shapes=[
            pltpu.VMEM((66, 8, 128), BF16),
            pltpu.SemaphoreType.DMA((2,)),
            pltpu.SemaphoreType.DMA((2,)),
            pltpu.SemaphoreType.DMA,
            pltpu.SemaphoreType.DMA,
        ],
        compiler_params=pltpu.CompilerParams(collective_id=0, has_side_effects=True),
        name="exchange",
    )(volume)


def convolve(gathered, *raw):
    consts = tables()
    return pl.pallas_call(
        conv_kernel,
        out_shape=jax.ShapeDtypeStruct((DEPTH, 48, 128), BF16),
        in_specs=[VMEM] * 19,
        out_specs=VMEM,
        scratch_shapes=[
            pltpu.VMEM((256, 72), BF16),
            pltpu.VMEM((256, 128), F32),
            pltpu.VMEM((192, 512), BF16),
            pltpu.VMEM((192, 128), F32),
            pltpu.VMEM((96, 192), BF16),
            pltpu.VMEM((96, 128), F32),
            pltpu.VMEM((144, 288), BF16),
            pltpu.VMEM((48, 128), F32),
            pltpu.VMEM((HALF, 48, 128), F32),
            pltpu.VMEM((HALF, 48, 128), F32),
        ],
        compiler_params=pltpu.CompilerParams(vmem_limit_bytes=40 * 1024 * 1024),
        name="convolve",
    )(gathered, *raw, *consts)


def shards(volume, w1, o1, w2, o2, w3, o3, w4, o4):
    gathered = exchange(volume)
    done = convolve(
        gathered, w1, o1[None], w2, o2[None], w3, o3[None], w4.reshape(3, 216, 24), o4[None]
    )
    return done.reshape(DEPTH, 24, 2, 128)


def solution(mesh):
    return jax.shard_map(
        shards,
        mesh=mesh,
        in_specs=(P("zs", "vol", None), P(), P(), P(), P(), P(), P(), P(), P()),
        out_specs=P(None, None, ("vol", "zs"), None),
        check_vma=False,
    )
```

time: 201 us -> 64.2 us (0.32)
  matrix products: 87 us -> 0 us
  Pallas kernels: 0 us -> 56 us
  local copies, waits for them, and re-layouts: 44.5 us -> 7.52 us
  starting transfers between devices: 29.8 us -> 0 us
  waiting for transfers between devices: 23.5 us -> 0 us
  other arithmetic: 15.4 us -> 0 us
    dot_general x37 -> x0, matrix products: 87 us -> none  [the longest x27 48.3 us: deep_conv(): jnp.einsum('zcxy,cd->zdxy', window, deep_weight[9 * along_z + 3 * along_x...]
    pallas_call x0 -> x2, Pallas kernels: none -> 56 us  [the longest x1 31.6 us: convolve(): pl.pallas_call(conv_kernel, out_shape=jax.ShapeDtypeStruct((DEPTH, 48, 12...]
    all_to_all x1 -> x0, waiting for transfers between devices: 20 us -> none  [shards(): lax.all_to_all(resident_reduced, 'zs', split_axis=2, concat_axis=0, tiled...]
    ppermute x4 -> x0, starting transfers between devices: 17.9 us -> none  [the longest x2 9.13 us: extended(): before = lax.ppermute(last, axis, up)]
    unnamed x55 -> x36, local copies, waits for them, and re-layouts: 25.3 us -> 7.52 us
    convert_element_type x2 -> x0, local copies, waits for them, and re-layouts: 14.3 us -> none  [the longest x1 12.8 us: leading_section(): jax.nn.relu(plane_conv(first, second_weight, second_offset))]
    all_to_all x1 -> x0, starting transfers between devices: 11.9 us -> none  [shards(): lax.all_to_all(resident_reduced, 'zs', split_axis=2, concat_axis=0, tiled...]
    convert_element_type x1 -> x0, other arithmetic: 9.01 us -> none  [leading_section(): first = jnp.where(outside, 0.0, first).astype(jnp.bfloat16)]
  transfers between devices with their start and end apart: 5 -> 0, of which waited for: 2 -> 0; matrix products, arithmetic and copies ran while one was open for 15% -> 0% of each run, Pallas kernels for 0% -> 0%
where the time goes in v1:
time: 64.2 us; the launch traced here: 63.7 us
  Pallas kernels  56 us (87%)
  local copies, waits for them, and re-layouts  7.52 us (12%)
    pallas_call x1, Pallas kernels, convolve(): pl.pallas_call(conv_kernel, out_shape=jax.ShapeDtypeStruct((DEPTH, 48, 12...  31.6 us
    pallas_call x1, Pallas kernels, exchange(): pl.pallas_call(exchange_kernel, out_shape=jax.ShapeDtypeStruct((DEPTH, 3,...  24.4 us
    unnamed x36, local copies, waits for them, and re-layouts  7.52 us

profile of v1, /device:TPU:1, one launch (start us, length us, event | category | flops | bytes accessed | tf_op | source)
XLA Modules:
  0.0 63.7 jit_solution(1565369968778292773)
XLA Ops:
  0.0 0.7 %copy.21.refs_5_ = bf16[4,12,24]{2,1,0:T(8,128)(2,1)S(1)} copy(bf16[4,12,24]{2,0,1:T(4,128)(2,1)} %param.24) | data formatting | bytes 4608 | tf_op args[5]
  0.8 1.2 %copy.20 = bf16[27,24,24]{2,1,0:T(8,128)(2,1)S(1)} copy(bf16[27,24,24]{0,2,1:T(8,128)(2,1)} %param.26) | data formatting | bytes 62208 | tf_op args[7]
  2.0 0.0 copy-start.1
  2.0 0.0 copy-start.2
  2.0 0.0 copy-start.13
  2.0 0.0 copy-start.14
  2.0 0.0 copy-start.15
  2.0 0.0 copy-start.16
  2.0 24.4 %exchange.1.refs_0_ = bf16[64,3,8,128]{3,2,1,0:T(8,128)(2,1)} custom-call(bf16[1,256,256]{2,1,0:T(8,128)(2,1)} %volume_ref.1), custom_call_target="tpu_custom_call" | custom-call | tf_op jit(solution)/shard_map/exchange/pallas_call | solution.py:329
  26.4 0.0 copy-done.11
  26.5 0.0 copy-done.5
  26.5 0.0 copy-done.3
  26.5 0.0 copy-done.4
  26.5 0.0 copy-done.1
  26.5 0.0 copy-done.2
  26.5 0.0 copy-done.13
  26.6 1.0 %copy-done = bf16[64,3,8,128]{3,2,1,0:T(8,128)(2,1)S(1)} copy-done((bf16[64,3,8,128]{3,2,1,0:T(8,128)(2,1)S(1)}, bf16[64,3,8,128]{3,2,1,0:T(8,128)(2,1)}, u32[]{:S(2)}) %copy-start) | copy-done | bytes 393240
  27.5 0.8 %copy-done.6 = bf16[180,72]{1,0:T(8,128)(2,1)S(1)} copy-done((bf16[180,72]{1,0:T(8,128)(2,1)S(1)}, bf16[180,72]{1,0:T(8,128)(2,1)}, u32[]{:S(2)}) %copy-start.6) | copy-done | bytes 25944
  28.3 0.8 %copy-done.7 = bf16[180,9]{1,0:T(8,128)(2,1)S(1)} copy-done((bf16[180,9]{1,0:T(8,128)(2,1)S(1)}, bf16[180,9]{1,0:T(8,128)(2,1)}, u32[]{:S(2)}) %copy-start.7) | copy-done | bytes 3264
  29.1 0.8 %copy-done.8 = bf16[9,12,12]{2,1,0:T(8,128)(2,1)S(1)} copy-done((bf16[9,12,12]{2,1,0:T(8,128)(2,1)S(1)}, bf16[9,12,12]{2,1,0:T(8,128)(2,1)}, u32[]{:S(2)}) %copy-start.8) | copy-done | bytes 2616
  29.9 0.8 %copy-done.9 = bf16[4,12,256]{2,1,0:T(8,128)(2,1)S(1)} copy-done((bf16[4,12,256]{2,1,0:T(8,128)(2,1)S(1)}, bf16[4,12,256]{2,1,0:T(8,128)(2,1)}, u32[]{:S(2)}) %copy-start.9) | copy-done | bytes 24600
  30.7 0.7 %copy-done.10 = bf16[96,12]{1,0:T(8,128)(2,1)S(1)} copy-done((bf16[96,12]{1,0:T(8,128)(2,1)S(1)}, bf16[96,12]{1,0:T(8,128)(2,1)}, u32[]{:S(2)}) %copy-start.10) | copy-done | bytes 2328
  31.4 0.7 %copy-done.12 = bf16[9,12]{1,0:T(8,128)(2,1)S(1)} copy-done((bf16[9,12]{1,0:T(8,128)(2,1)S(1)}, bf16[9,12]{1,0:T(8,128)(2,1)}, u32[]{:S(2)}) %copy-start.12) | copy-done | bytes 240
  32.1 31.6 %convolve.1 = bf16[64,48,128]{2,1,0:T(8,128)(2,1)} custom-call(bf16[64,3,8,128]{3,2,1,0:T(8,128)(2,1)S(1)} %copy-done, bf16[9,12]{1,0:T(8,128)(2,1)S(1)} %copy-done.12, f32[1,12]{1,0:T(1,128)S(1)} %bitcast.7, bf16[9,12,12]{2,1,0:T(8,128)(2,1)S(1)} %copy-done.8, f32[1,12]{1,0:T(1,128)S(1)} %bitcast.8, bf16[4,12,24]{2,1,0:T(8,128)(2,1)S(1)} %copy.21.refs_5_, ...), custom_call_target="tpu_custom_call" | custom-call | tf_op jit(solution)/shard_map/convolve/pallas_call | solution.py:348
  (14 shorter events, 0.0 us)
Async XLA Ops:
  0.0 26.4 %copy-start.11 = (bf16[48,24]{1,0:T(8,128)(2,1)S(1)}, bf16[48,24]{1,0:T(8,128)(2,1)}, u32[]{:S(2)}) copy-start(bf16[48,24]{1,0:T(8,128)(2,1)} %constant.28.clone.refs_17_) | copy-start | bytes 6916
  0.0 26.4 %copy-start.5 = (bf16[3,96,24]{2,1,0:T(8,128)(2,1)S(1)}, bf16[3,96,24]{2,1,0:T(8,128)(2,1)}, u32[]{:S(2)}) copy-start(bf16[3,96,24]{2,1,0:T(8,128)(2,1)} %constant.26.clone.refs_15_) | copy-start | bytes 41476
  0.7 25.7 %copy-start.3 = (bf16[216,384]{1,0:T(8,128)(2,1)S(1)}, bf16[216,384]{1,0:T(8,128)(2,1)}, u32[]{:S(2)}) copy-start(bf16[216,384]{1,0:T(8,128)(2,1)} %constant.29.clone.refs_18_) | copy-start | bytes 497668
  0.8 25.7 %copy-start.4 = (bf16[256,180]{1,0:T(8,128)(2,1)S(1)}, bf16[256,180]{1,0:T(8,128)(2,1)}, u32[]{:S(2)}) copy-start(bf16[256,180]{1,0:T(8,128)(2,1)} %constant.21.clone.refs_10_) | copy-start | bytes 276484
  2.0 24.5 %copy-start.1 = (bf16[9,12,1024]{2,1,0:T(8,128)(2,1)S(1)}, bf16[9,12,1024]{2,1,0:T(8,128)(2,1)}, u32[]{:S(2)}) copy-start(bf16[9,12,1024]{2,1,0:T(8,128)(2,1)} %constant.25.clone.refs_14_) | copy-start | bytes 663556
  2.0 24.5 %copy-start.2 = (bf16[3,256,12]{2,1,0:T(8,128)(2,1)S(1)}, bf16[3,256,12]{2,1,0:T(8,128)(2,1)}, u32[]{:S(2)}) copy-start(bf16[3,256,12]{2,1,0:T(8,128)(2,1)} %constant.20.clone.refs_9_) | copy-start | bytes 55300
  2.0 24.5 %copy-start.13 = (f32[12]{0:T(128)S(1)}, f32[12]{0:T(128)}, u32[]{:S(2)}) copy-start(f32[12]{0:T(128)} %param.21) | copy-start | bytes 148
  2.0 24.5 %copy-start.14 = (f32[12]{0:T(128)S(1)}, f32[12]{0:T(128)}, u32[]{:S(2)}) copy-start(f32[12]{0:T(128)} %param.23) | copy-start | bytes 148
  2.0 24.5 %copy-start.15 = (f32[24]{0:T(128)S(1)}, f32[24]{0:T(128)}, u32[]{:S(2)}) copy-start(f32[24]{0:T(128)} %param.25) | copy-start | bytes 292
  2.0 24.5 %copy-start.16 = (f32[24]{0:T(128)S(1)}, f32[24]{0:T(128)}, u32[]{:S(2)}) copy-start(f32[24]{0:T(128)} %param.27) | copy-start | bytes 292
  26.5 1.0 %copy-start = (bf16[64,3,8,128]{3,2,1,0:T(8,128)(2,1)S(1)}, bf16[64,3,8,128]{3,2,1,0:T(8,128)(2,1)}, u32[]{:S(2)}) copy-start(bf16[64,3,8,128]{3,2,1,0:T(8,128)(2,1)} %exchange.1.refs_0_) | copy-start | bytes 1179652
  27.5 0.8 %copy-start.6 = (bf16[180,72]{1,0:T(8,128)(2,1)S(1)}, bf16[180,72]{1,0:T(8,128)(2,1)}, u32[]{:S(2)}) copy-start(bf16[180,72]{1,0:T(8,128)(2,1)} %constant.23.clone.refs_12_) | copy-start | bytes 77764
  28.3 0.8 %copy-start.7 = (bf16[180,9]{1,0:T(8,128)(2,1)S(1)}, bf16[180,9]{1,0:T(8,128)(2,1)}, u32[]{:S(2)}) copy-start(bf16[180,9]{1,0:T(8,128)(2,1)} %constant.22.clone.refs_11_) | copy-start | bytes 9724
  29.1 0.8 %copy-start.8 = (bf16[9,12,12]{2,1,0:T(8,128)(2,1)S(1)}, bf16[9,12,12]{2,1,0:T(8,128)(2,1)}, u32[]{:S(2)}) copy-start(bf16[9,12,12]{2,1,0:T(8,128)(2,1)} %refs_3_.1) | copy-start | bytes 7780
  29.9 0.8 %copy-start.9 = (bf16[4,12,256]{2,1,0:T(8,128)(2,1)S(1)}, bf16[4,12,256]{2,1,0:T(8,128)(2,1)}, u32[]{:S(2)}) copy-start(bf16[4,12,256]{2,1,0:T(8,128)(2,1)} %constant.27.clone.refs_16_) | copy-start | bytes 73732
  30.7 0.7 %copy-start.10 = (bf16[96,12]{1,0:T(8,128)(2,1)S(1)}, bf16[96,12]{1,0:T(8,128)(2,1)}, u32[]{:S(2)}) copy-start(bf16[96,12]{1,0:T(8,128)(2,1)} %constant.24.clone.refs_13_) | copy-start | bytes 6916
  31.4 0.7 %copy-start.12 = (bf16[9,12]{1,0:T(8,128)(2,1)S(1)}, bf16[9,12]{1,0:T(8,128)(2,1)}, u32[]{:S(2)}) copy-start(bf16[9,12]{1,0:T(8,128)(2,1)} %refs_1_.1) | copy-start | bytes 652

commit v2 on v1

v2 whole, which is shorter than its diff:
```python
import functools

import jax
import jax.numpy as jnp
import numpy as np
from jax import lax
from jax.experimental import pallas as pl
from jax.experimental.pallas import tpu as pltpu
from jax.sharding import PartitionSpec as P

BF16 = jnp.bfloat16
F32 = jnp.float32
MESH = pl.DeviceIdType.MESH
DEPTH = 64
HALF = DEPTH // 2


def tables():
    place1 = np.zeros((3, 256, 12), np.float32)
    mask1 = np.zeros((256, 180), np.float32)
    pick1 = np.zeros((180, 9), np.float32)
    lay1 = np.zeros((180, 72), np.float32)
    source = ({0: (0, 1), 1: (1, 0), 2: (1, 1)}, {0: (1, 0), 1: (1, 1), 2: (2, 0)})
    for parity in range(2):
        for row in range(10):
            kind = parity * 10 + row
            for chan in range(12):
                at = parity * 128 + chan * 10 + row
                place1[0, at, chan] = 1
                place1[1, at, chan] = row >= 3
                place1[2, at, chan] = row < 7
                mask1[at, kind * 9 : kind * 9 + 9] = 1
            for along_x in range(3):
                for along_y in range(3):
                    tap = 3 * along_x + along_y
                    pick1[kind * 9 + tap, tap] = 1
                    shift, origin = source[parity][along_y]
                    fine = row + along_x
                    column = shift * 24 + (fine // 4) * 8 + origin * 4 + fine % 4
                    lay1[kind * 9 + tap, column] = 1
    place2 = np.zeros((96, 12), np.float32)
    lay2 = np.zeros((9, 12, 1024), np.float32)
    block = ({0: 0, 1: 1, 2: 2}, {0: 1, 1: 2, 2: 3})
    for chan in range(12):
        place2[chan * 8 : chan * 8 + 8, chan] = 1
        for along_x in range(3):
            for along_y in range(3):
                for parity in range(2):
                    column = parity * 512 + block[parity][along_y] * 128 + chan * 10 + along_x
                    lay2[3 * along_x + along_y, chan, column] = 1
    place3 = np.zeros((3, 96, 24), np.float32)
    for chan in range(24):
        for row in range(4):
            place3[0, chan * 4 + row, chan] = 1
            place3[1, chan * 4 + row, chan] = row >= 1
            place3[2, chan * 4 + row, chan] = row < 3
    lay3 = np.zeros((12, 4, 256), np.float32)
    for a in range(2):
        for b in range(2):
            for chan in range(12):
                lay3[chan, 2 * a + b, b * 96 + chan * 8 + a] = 1
    place4 = np.zeros((48, 24), np.float32)
    lay4 = np.zeros((24, 27, 1152), np.float32)
    for chan in range(24):
        place4[chan * 2 : chan * 2 + 2, chan] = 1
        for along_z in range(3):
            for along_x in range(3):
                for along_y in range(3):
                    tap = 9 * along_z + 3 * along_x + along_y
                    lay4[chan, tap, along_z * 384 + along_y * 96 + chan * 4 + along_x] = 1
    made = (place1, mask1, pick1, lay1, place2, lay2, place3, lay3, place4, lay4)
    return [table.astype(jnp.bfloat16) for table in made]


def mul(a, b):
    return jnp.dot(a, b, preferred_element_type=F32)


def mul_t(a, b):
    return lax.dot_general(a, b, (((1,), (1,)), ((), ())), preferred_element_type=F32)


def column(place, offset):
    summed = jnp.sum(place.astype(F32) * offset, axis=1, keepdims=True)
    return jnp.broadcast_to(summed, (place.shape[0], 128))


def lay_weights(edge, raw, consts, laid):
    w1_ref, o1_ref, w2_ref, o2_ref, w3_ref, o3_ref, w4_ref, o4_ref = raw
    place1, mask1, pick1, lay1, place2, lay2, place3, lay3, place4, lay4 = consts
    m1, b1, m2, b2, m3, b3, m4, b4 = laid

    here1, here2, here3 = place1[edge], place2[...], place3[edge]
    taps1 = mul(pick1[...], w1_ref[...]).astype(BF16)
    taps2 = [mul_t(here2, w2_ref[tap]).astype(BF16) for tap in range(9)]
    taps3 = [mul_t(here3, w3_ref[chan]).astype(BF16) for chan in range(12)]
    wide4 = sum(mul(w4_ref[chan], lay4[chan]) for chan in range(24)).astype(BF16)

    chosen = mul_t(here1, taps1) * mask1[...].astype(F32)
    base2 = sum(mul(taps2[tap], lay2[tap]) for tap in range(9))
    base3 = sum(mul(taps3[chan], lay3[chan]) for chan in range(12))
    base4 = mul(place4[...], wide4)

    m1[...] = mul(chosen.astype(BF16), lay1[...]).astype(BF16)
    for parity in range(2):
        for block in range(4):
            start = parity * 512 + block * 128
            rows = [
                pltpu.roll(base2[8 * c : 8 * c + 8, start : start + 128], 0, 1, stride=1, stride_axis=0)
                for c in range(12)
            ]
            m2[96 * parity : 96 * parity + 96, 128 * block : 128 * block + 128] = jnp.concatenate(
                rows, axis=0
            ).astype(BF16)
    row = lax.broadcasted_iota(jnp.int32, base3.shape, 0) & 3
    placed = base3
    for r in range(1, 4):
        placed = jnp.where(row == r, pltpu.roll(base3, 2 * r, 1), placed)
    m3[...] = placed[:, :192].astype(BF16)
    row = lax.broadcasted_iota(jnp.int32, base4.shape, 0) & 1
    placed = jnp.where(row == 1, pltpu.roll(base4, 1, 1), base4)
    for dz in range(3):
        m4[48 * dz : 48 * dz + 48] = placed[:, 384 * dz : 384 * dz + 288].astype(BF16)

    b1[...] = column(here1, o1_ref[...])
    offset2 = column(here2, o2_ref[...])
    b2[:96] = offset2
    b2[96:] = offset2
    b3[...] = column(here3, o3_ref[...])
    b4[...] = column(place4[...], o4_ref[...])


def from_left(value, lane):
    return jnp.where(lane == 0, 0.0, pltpu.roll(value, 1, 1))


def from_right(value, lane):
    return jnp.where(lane == 127, 0.0, pltpu.roll(value, 127, 1))


def both(function, value):
    lane = lax.broadcasted_iota(jnp.int32, (value.shape[0], 128), 1)
    return jnp.concatenate([function(value[:, :128], lane), function(value[:, 128:], lane)], axis=1)


def twice(bias):
    return jnp.concatenate([bias, bias], axis=1)


def relu(value):
    return jnp.maximum(value, 0.0)


def convolve_slices(me, arrive, x_ref, laid, held, out_ref):
    m1, b1, m2, b2, m3, b3, m4, b4 = laid
    start_ref, first_ref, second_ref, coarse_ref = held
    groups = HALF // 2

    def step(turn, carry):
        arrive(turn)
        group = jnp.maximum(turn - 3, 0)
        closing, opening = [jnp.where(turn > 3, part, 0.0) for part in carry]
        deep = [mul(m4[...], coarse_ref[half]) for half in range(2)]

        def joined(half, part):
            z = lax.rem(me + 2 * group + half, DEPTH)
            return jnp.concatenate(
                [jnp.where(z == 0, 0.0, part[:, :128]), jnp.where(z == HALF, 0.0, part[:, 128:])], axis=1
            )

        into_before = joined(0, deep[0][96:])
        before = closing + into_before
        here = joined(0, opening) + deep[0][48:96] + joined(1, deep[1][96:])
        start_ref[group, 0] = into_before
        start_ref[group, 1] = here
        bias = twice(b4[...])
        for shift, total in ((DEPTH - 1, before), (0, here)):
            done = relu(total + bias).astype(BF16)
            out_ref[lax.rem(me + 2 * group + shift, DEPTH)] = done[:, :128]
            out_ref[lax.rem(me + 2 * group + shift + HALF, DEPTH)] = done[:, 128:]
        carry = joined(1, deep[0][:48]) + deep[1][48:96], deep[1][:48]

        for half in range(2):
            coarse = relu(mul(m3[...], second_ref[half]) + twice(b3[...]))
            coarse_ref[half, :96] = both(from_left, coarse).astype(BF16)
            coarse_ref[half, 96:192] = coarse.astype(BF16)
            coarse_ref[half, 192:] = both(from_right, coarse).astype(BF16)

        for half in range(2):
            second = relu(mul(m2[...], first_ref[half]) + twice(b2[...]))
            second_ref[half] = second.astype(BF16)

        for half in range(2):
            low = lax.rem(me + 2 * jnp.minimum(turn, groups - 1) + half, DEPTH)
            high = lax.rem(low + HALF, DEPTH)
            field = jnp.concatenate(
                [x_ref[low].astype(F32).reshape(24, 128), x_ref[high].astype(F32).reshape(24, 128)], axis=1
            )
            stacked = jnp.concatenate([both(from_left, field), field, both(from_right, field)], axis=0)
            first = relu(mul(m1[...], stacked.astype(BF16)) + twice(b1[...]))
            even, odd = first[:128], first[128:]
            first_ref[half, :128] = both(from_left, odd).astype(BF16)
            first_ref[half, 128:256] = even.astype(BF16)
            first_ref[half, 256:384] = odd.astype(BF16)
            first_ref[half, 384:] = both(from_right, even).astype(BF16)
        return carry

    zero = jnp.zeros((48, 256), F32)
    closing, opening = lax.fori_loop(0, groups + 3, step, (zero, zero))
    bias = b4[...]
    swap = lambda value: jnp.concatenate([value[:, 128:], value[:, :128]], axis=1)
    opening = swap(opening)
    opening = jnp.concatenate(
        [jnp.where(me == 0, 0.0, opening[:, :128]), jnp.where(me == HALF, 0.0, opening[:, 128:])], axis=1
    )
    ends = ((HALF - 1, closing + swap(start_ref[0, 0])), (0, start_ref[0, 1] + opening))
    for shift, total in ends:
        done = relu(total + twice(bias)).astype(BF16)
        out_ref[lax.rem(me + shift, DEPTH)] = done[:, :128]
        out_ref[lax.rem(me + shift + HALF, DEPTH)] = done[:, 128:]


EARLY = 8


def encoder_kernel(*refs):
    volume_hbm, fetched_hbm, out_ref = refs[0], refs[1:19], refs[19]
    volume_ref, fetched = refs[20], refs[21:39]
    laid, held = refs[39:47], refs[47:51]
    tiles, got_ref = refs[51:53]
    fetch_sem, halo_send, halo_recv, send_sem, recv_sem = refs[53:]
    vol, me = lax.axis_index("vol"), lax.axis_index("zs")
    vols, members = lax.axis_size("vol"), lax.axis_size("zs")

    load = pltpu.make_async_copy(volume_hbm, volume_ref, fetch_sem.at[18])
    load.start()
    loads = [
        pltpu.make_async_copy(source, target, fetch_sem.at[at])
        for at, (source, target) in enumerate(zip(fetched_hbm, fetched))
    ]
    barrier = pltpu.get_barrier_semaphore()

    def greet(step, carry):
        pl.semaphore_signal(
            barrier, inc=1, device_id=(vol, lax.rem(me + step, members)), device_id_type=MESH
        )
        return carry

    @pl.when(vol > 0)
    def _():
        pl.semaphore_signal(barrier, inc=1, device_id=(vol - 1, me), device_id_type=MESH)

    @pl.when(vol < vols - 1)
    def _():
        pl.semaphore_signal(barrier, inc=1, device_id=(vol + 1, me), device_id_type=MESH)

    lax.fori_loop(1, members, greet, 0)
    for each in loads:
        each.start()
    load.wait()

    line = lax.broadcasted_iota(jnp.int32, (256, 256), 0)
    lane = lax.broadcasted_iota(jnp.int32, (256, 256), 1)
    parted = (line == jnp.where(lane < 128, 2 * lane, 2 * lane - 255)).astype(F32).astype(BF16)
    split = mul(volume_ref[0], parted)
    even = split[:, :128].reshape(32, 8, 128)
    odd = split[:, 128:].reshape(32, 8, 128)
    row = lax.broadcasted_iota(jnp.int32, (32, 8, 128), 1)
    upper = jnp.where(row < 4, even, pltpu.roll(odd, 4, 1))
    lower = jnp.where(row < 4, pltpu.roll(even, 4, 1), odd)
    tiles[1:65] = jnp.stack([upper, lower], axis=1).reshape(64, 8, 128).astype(BF16)

    @pl.when(vol == 0)
    def _():
        tiles[0] = jnp.zeros((8, 128), BF16)

    @pl.when(vol == vols - 1)
    def _():
        tiles[65] = jnp.zeros((8, 128), BF16)

    for each in loads:
        each.wait()
    edge = jnp.where(
        (vol == 0) & (me == 0), 1, jnp.where((vol == vols - 1) & (me == members - 1), 2, 0)
    )
    lay_weights(edge, fetched[:8], fetched[8:], laid)

    pl.semaphore_wait(
        barrier, members - 1 + jnp.where(vol > 0, 1, 0) + jnp.where(vol < vols - 1, 1, 0)
    )

    def upward():
        return pltpu.make_async_remote_copy(
            src_ref=tiles.at[1],
            dst_ref=tiles.at[65],
            send_sem=halo_send.at[0],
            recv_sem=halo_recv.at[0],
            device_id=(vol - 1, me),
            device_id_type=MESH,
        )

    def downward():
        return pltpu.make_async_remote_copy(
            src_ref=tiles.at[64],
            dst_ref=tiles.at[0],
            send_sem=halo_send.at[1],
            recv_sem=halo_recv.at[1],
            device_id=(vol + 1, me),
            device_id_type=MESH,
        )

    @pl.when(vol > 0)
    def _():
        upward().start()

    @pl.when(vol < vols - 1)
    def _():
        downward().start()

    def give(target):
        pltpu.make_async_remote_copy(
            src_ref=tiles.at[pl.ds(target, 3)],
            dst_ref=got_ref.at[me],
            send_sem=send_sem,
            recv_sem=recv_sem.at[me],
            device_id=(vol, target),
            device_id_type=MESH,
        ).start()

    own = pltpu.make_async_copy(tiles.at[pl.ds(me, 3)], got_ref.at[me], recv_sem.at[me])
    at_edge = (me == 0) | (me == members - 1)

    @pl.when(jnp.logical_not(at_edge))
    def _():
        own.start()

    def targets(step):
        near = lax.rem(me - step + members, members)
        return near, lax.rem(near + HALF, members)

    def send_early(step, carry):
        for target in targets(step):
            @pl.when((target != 0) & (target != members - 1) & (target != me))
            def _():
                give(target)
        return carry

    def send_late(step, carry):
        for target in targets(step):
            give(target)
        return carry

    lax.fori_loop(0, EARLY, send_early, 0)

    @pl.when(vol < vols - 1)
    def _():
        upward().wait_recv()

    @pl.when(vol > 0)
    def _():
        downward().wait_recv()

    @pl.when(at_edge)
    def _():
        own.start()

    for target in (0, members - 1):
        @pl.when((lax.rem(me - target + members, HALF) < EARLY) & (me != target))
        def _():
            give(target)

    lax.fori_loop(EARLY, HALF, send_late, 0)

    def arrive(turn):
        @pl.when(turn < HALF // 2)
        def _():
            for half in range(2):
                for shift in (0, HALF):
                    z = lax.rem(me + 2 * turn + half + shift, DEPTH)
                    pltpu.make_async_copy(got_ref.at[z], got_ref.at[z], recv_sem.at[z]).wait()

    convolve_slices(me, arrive, got_ref, laid, held, out_ref)

    @pl.when(vol > 0)
    def _():
        upward().wait_send()

    @pl.when(vol < vols - 1)
    def _():
        downward().wait_send()

    rest = got_ref.at[pl.ds(0, 63)]
    pltpu.make_async_copy(rest, rest, send_sem).wait()


def encode(volume, *raw):
    fetched = (*raw, *tables())
    return pl.pallas_call(
        encoder_kernel,
        out_shape=jax.ShapeDtypeStruct((DEPTH, 48, 128), BF16),
        in_specs=[pl.BlockSpec(memory_space=pltpu.HBM)] * 19,
        out_specs=pl.BlockSpec(memory_space=pltpu.VMEM),
        scratch_shapes=[
            pltpu.VMEM(volume.shape, BF16),
            *[pltpu.VMEM(value.shape, value.dtype) for value in fetched],
            pltpu.VMEM((256, 72), BF16),
            pltpu.VMEM((256, 128), F32),
            pltpu.VMEM((192, 512), BF16),
            pltpu.VMEM((192, 128), F32),
            pltpu.VMEM((96, 192), BF16),
            pltpu.VMEM((96, 128), F32),
            pltpu.VMEM((144, 288), BF16),
            pltpu.VMEM((48, 128), F32),
            pltpu.VMEM((HALF // 2, 2, 48, 256), F32),
            pltpu.VMEM((2, 512, 256), BF16),
            pltpu.VMEM((2, 192, 256), BF16),
            pltpu.VMEM((2, 288, 256), BF16),
            pltpu.VMEM((66, 8, 128), BF16),
            pltpu.VMEM((DEPTH, 3, 8, 128), BF16),
            pltpu.SemaphoreType.DMA((19,)),
            pltpu.SemaphoreType.DMA((2,)),
            pltpu.SemaphoreType.DMA((2,)),
            pltpu.SemaphoreType.DMA,
            pltpu.SemaphoreType.DMA((DEPTH,)),
        ],
        compiler_params=pltpu.CompilerParams(
            collective_id=0, has_side_effects=True, vmem_limit_bytes=56 * 1024 * 1024
        ),
        name="encode",
    )(volume, *fetched)


def shards(volume, w1, o1, w2, o2, w3, o3, w4, o4):
    done = encode(
        volume,
        w1,
        o1[None],
        w2,
        o2[None],
        w3.transpose(1, 0, 2),
        o3[None],
        w4.transpose(1, 2, 0),
        o4[None],
    )
    return done.reshape(DEPTH, 24, 2, 128)


def solution(mesh):
    return jax.shard_map(
        shards,
        mesh=mesh,
        in_specs=(P("zs", "vol", None), P(), P(), P(), P(), P(), P(), P(), P()),
        out_specs=P(None, None, ("vol", "zs"), None),
        check_vma=False,
    )
```

time: 64.2 us -> 33.9 us (0.53)
  Pallas kernels: 56 us -> 31.2 us
  local copies, waits for them, and re-layouts: 7.52 us -> 2.55 us
    pallas_call x2 -> x1, Pallas kernels: 56 us -> 31.2 us  [encode(): pl.pallas_call(encoder_kernel, out_shape=jax.ShapeDtypeStruct((DEPTH, 48,...]
    unnamed x36 -> x1, local copies, waits for them, and re-layouts: 7.52 us -> 2.55 us
where the time goes in v2:
time: 33.9 us; the launch traced here: 33.8 us
  Pallas kernels  31.2 us (92%)
  local copies, waits for them, and re-layouts  2.55 us (8%)
    pallas_call x1, Pallas kernels, encode(): pl.pallas_call(encoder_kernel, out_shape=jax.ShapeDtypeStruct((DEPTH, 48,...  31.2 us
    unnamed x1, local copies, waits for them, and re-layouts  2.55 us

profile of v2, /device:TPU:1, one launch (start us, length us, event | category | flops | bytes accessed | tf_op | source)
XLA Modules:
  0.0 33.8 jit_solution(9927024516515528126)
XLA Ops:
  0.0 31.2 %encode.1 = bf16[64,48,128]{2,1,0:T(8,128)(2,1)} custom-call(bf16[1,256,256]{2,1,0:T(8,128)(2,1)} %refs_0_.1, bf16[9,12]{1,0:T(8,128)(2,1)} %refs_1_.1, f32[1,12]{1,0:T(1,128)} %bitcast.10, bf16[9,12,12]{2,1,0:T(8,128)(2,1)} %refs_3_.1, f32[1,12]{1,0:T(1,128)} %bitcast.11, bf16[12,4,24]{2,1,0:T(4,128)(2,1)} %bitcast.9, f32[1,24]{1,0:T(1,128)} %bitcast.12, ...), custom_call_target="tpu_custom_call" | custom-call | tf_op jit(solution)/shard_map/encode/pallas_call | solution.py:398
  31.2 2.6 %copy.21 = bf16[64,24,2,128]{3,2,1,0:T(2,128)(2,1)} copy(bf16[64,24,2,128]{3,2,1,0:T(2,128)(2,1)} %bitcast.7) | data formatting | bytes 1572864

commit v3 on v2

v3 whole, which is shorter than its diff:
```python
import functools

import jax
import jax.numpy as jnp
import numpy as np
from jax import lax
from jax.experimental import pallas as pl
from jax.experimental.pallas import tpu as pltpu
from jax.sharding import PartitionSpec as P

BF16 = jnp.bfloat16
F32 = jnp.float32
MESH = pl.DeviceIdType.MESH
DEPTH = 64
HALF = DEPTH // 2


def tables():
    place1 = np.zeros((3, 256, 12), np.float32)
    mask1 = np.zeros((256, 180), np.float32)
    pick1 = np.zeros((180, 9), np.float32)
    lay1 = np.zeros((180, 80), np.float32)
    source = ({0: (0, 1), 1: (1, 0), 2: (1, 1)}, {0: (1, 0), 1: (1, 1), 2: (2, 0)})
    for parity in range(2):
        for row in range(10):
            kind = parity * 10 + row
            for chan in range(12):
                at = parity * 128 + chan * 10 + row
                place1[0, at, chan] = 1
                place1[1, at, chan] = row >= 3
                place1[2, at, chan] = row < 7
                mask1[at, kind * 9 : kind * 9 + 9] = 1
            for along_x in range(3):
                for along_y in range(3):
                    tap = 3 * along_x + along_y
                    pick1[kind * 9 + tap, tap] = 1
                    shift, origin = source[parity][along_y]
                    fine = row + along_x
                    column = shift * 24 + (fine // 4) * 8 + origin * 4 + fine % 4
                    lay1[kind * 9 + tap, column] = 1
    place2 = np.zeros((96, 12), np.float32)
    lay2 = np.zeros((9, 12, 1024), np.float32)
    block = ({0: 0, 1: 1, 2: 2}, {0: 1, 1: 2, 2: 3})
    for chan in range(12):
        place2[chan * 8 : chan * 8 + 8, chan] = 1
        for along_x in range(3):
            for along_y in range(3):
                for parity in range(2):
                    column = parity * 512 + block[parity][along_y] * 128 + chan * 10 + along_x
                    lay2[3 * along_x + along_y, chan, column] = 1
    place3 = np.zeros((3, 96, 24), np.float32)
    for chan in range(24):
        for row in range(4):
            place3[0, chan * 4 + row, chan] = 1
            place3[1, chan * 4 + row, chan] = row >= 1
            place3[2, chan * 4 + row, chan] = row < 3
    lay3 = np.zeros((12, 4, 256), np.float32)
    for a in range(2):
        for b in range(2):
            for chan in range(12):
                lay3[chan, 2 * a + b, b * 96 + chan * 8 + a] = 1
    place4 = np.zeros((48, 24), np.float32)
    lay4 = np.zeros((24, 27, 1152), np.float32)
    for chan in range(24):
        place4[chan * 2 : chan * 2 + 2, chan] = 1
        for along_z in range(3):
            for along_x in range(3):
                for along_y in range(3):
                    tap = 9 * along_z + 3 * along_x + along_y
                    lay4[chan, tap, along_z * 384 + along_y * 96 + chan * 4 + along_x] = 1
    made = (place1, mask1, pick1, lay1, place2, lay2, place3, lay3, place4, lay4)
    return [table.astype(jnp.bfloat16) for table in made]


def mul(a, b):
    return jnp.dot(a, b, preferred_element_type=F32)


def mul_t(a, b):
    return lax.dot_general(a, b, (((1,), (1,)), ((), ())), preferred_element_type=F32)


def column(place, offset):
    return jnp.sum(place.astype(F32) * offset, axis=1, keepdims=True)


def with_bias(weight, bias, start):
    high = bias.astype(BF16).astype(F32)
    middle = (bias - high).astype(BF16).astype(F32)
    low = bias - high - middle
    lane = lax.broadcasted_iota(jnp.int32, weight.shape, 1)
    for shift, part in enumerate((high, middle, low)):
        weight = jnp.where(lane == start + shift, part, weight)
    return weight.astype(BF16)


def lay_weights(edge, raw, consts, laid):
    w1_ref, o1_ref, w2_ref, o2_ref, w3_ref, o3_ref, w4_ref, o4_ref = raw
    place1, mask1, pick1, lay1, place2, lay2, place3, lay3, place4, lay4 = consts
    m1, m2, m3, b3, m4 = laid

    here1, here2, here3 = place1[edge], place2[...], place3[edge]
    taps1 = mul(pick1[...], w1_ref[...]).astype(BF16)
    taps2 = [mul_t(here2, w2_ref[tap]).astype(BF16) for tap in range(9)]
    taps3 = [mul_t(here3, w3_ref[chan]).astype(BF16) for chan in range(12)]
    wide4 = sum(mul(w4_ref[chan], lay4[chan]) for chan in range(24)).astype(BF16)

    chosen = mul_t(here1, taps1) * mask1[...].astype(F32)
    base2 = sum(mul(taps2[tap], lay2[tap]) for tap in range(9))
    base3 = sum(mul(taps3[chan], lay3[chan]) for chan in range(12))
    base4 = mul(place4[...], wide4)

    row = lax.broadcasted_iota(jnp.int32, (256, 1), 0) & 127
    bias1 = jnp.where(row >= 120, 1.0, column(here1, o1_ref[...]))
    m1[...] = with_bias(mul(chosen.astype(BF16), lay1[...]), bias1, 72)
    bias2 = column(here2, o2_ref[...])
    for parity in range(2):
        for block in range(4):
            start = parity * 512 + block * 128
            rows = [
                pltpu.roll(base2[8 * c : 8 * c + 8, start : start + 128], 0, 1, stride=1, stride_axis=0)
                for c in range(12)
            ]
            placed = jnp.concatenate(rows, axis=0)
            placed = with_bias(placed, bias2, 120) if block == 1 else placed.astype(BF16)
            m2[96 * parity : 96 * parity + 96, 128 * block : 128 * block + 128] = placed
    row = lax.broadcasted_iota(jnp.int32, base3.shape, 0) & 3
    placed = base3
    for r in range(1, 4):
        placed = jnp.where(row == r, pltpu.roll(base3, 2 * r, 1), placed)
    m3[...] = placed[:, :192].astype(BF16)
    row = lax.broadcasted_iota(jnp.int32, base4.shape, 0) & 1
    placed = jnp.where(row == 1, pltpu.roll(base4, 1, 1), base4)
    bias4 = column(place4[...], o4_ref[...])
    for dz in range(3):
        part = placed[:, 384 * dz : 384 * dz + 304]
        part = with_bias(part, bias4, 288) if dz == 1 else part.astype(BF16)
        m4[48 * dz : 48 * dz + 48] = part
    b3[...] = jnp.broadcast_to(column(here3, o3_ref[...]), (96, 128))


def from_left(value, lane):
    return jnp.where(lane == 0, jnp.zeros((), BF16), pltpu.roll(value, 1, 1))


def from_right(value, lane):
    return jnp.where(lane == 127, jnp.zeros((), BF16), pltpu.roll(value, 127, 1))


def both(function, value):
    lane = lax.broadcasted_iota(jnp.int32, (value.shape[0], 128), 1)
    return jnp.concatenate([function(value[:, :128], lane), function(value[:, 128:], lane)], axis=1)


def twice(bias):
    return jnp.concatenate([bias, bias], axis=1)


def relu(value):
    return jnp.maximum(value.astype(BF16), jnp.zeros((), BF16))


def swap(value):
    return jnp.concatenate([value[:, 128:], value[:, :128]], axis=1)


def place_first(x_ref, m1, first_ref, lows):
    for half, (low, high) in enumerate(lows):
        field = jnp.concatenate(
            [x_ref[low].astype(F32).reshape(24, 128), x_ref[high].astype(F32).reshape(24, 128)], axis=1
        )
        lane = lax.broadcasted_iota(jnp.int32, field.shape, 1) & 127
        before = jnp.concatenate(
            [pltpu.roll(field[:, :128], 1, 1), pltpu.roll(field[:, 128:], 1, 1)], axis=1
        )
        after = jnp.concatenate(
            [pltpu.roll(field[:, :128], 127, 1), pltpu.roll(field[:, 128:], 127, 1)], axis=1
        )
        before = jnp.where(lane == 0, 0.0, before)
        after = jnp.where(lane == 127, 0.0, after)
        stacked = jnp.concatenate([before, field, after, jnp.ones((8, 256), F32)], axis=0)
        first = relu(mul(m1[...], stacked.astype(BF16)))
        even, odd = first[:128], first[128:]
        first_ref[half, :128] = both(from_left, odd)
        first_ref[half, 128:256] = even
        first_ref[half, 256:384] = odd
        first_ref[half, 384:] = both(from_right, even)


def place_second(first_ref, m2, second_ref):
    for half in range(2):
        second_ref[half] = relu(mul(m2[...], first_ref[half]))


def place_coarse(second_ref, m3, b3, coarse_ref):
    for half in range(2):
        coarse = relu(mul(m3[...], second_ref[half]) + twice(b3[...]))
        coarse_ref[half, :96] = both(from_left, coarse)
        coarse_ref[half, 96:192] = coarse
        coarse_ref[half, 192:288] = both(from_right, coarse)


def convolve_slices(me, arrive, leave, x_ref, laid, held, out_ref):
    m1, m2, m3, b3, m4 = laid
    first_ref, second_ref, coarse_ref = held
    coarse_ref[:, 288:] = jnp.ones((2, 16, 256), BF16)
    groups = HALF // 2

    def up(step):
        return lax.rem(me + step, DEPTH)

    def down(step):
        return lax.rem(me - 1 - step + 2 * DEPTH, DEPTH)

    def stage1(turn):
        pairs = [(up(2 * turn + half), down(2 * turn + half)) for half in range(2)]
        place_first(x_ref, m1, first_ref, pairs)

    def stage2():
        place_second(first_ref, m2, second_ref)

    def stage3():
        place_coarse(second_ref, m3, b3, coarse_ref)

    def joined(step, part):
        low = jnp.where(up(step) == 0, 0.0, part[:, :128])
        return jnp.concatenate([low, jnp.where(down(step) == DEPTH - 1, 0.0, part[:, 128:])], axis=1)

    def emit(step, total):
        done = relu(total)
        out_ref[up(step)] = done[:, :128]
        out_ref[down(step)] = done[:, 128:]
        leave(up(step))
        leave(down(step))

    def stage4(group, carry):
        for half in range(2):
            step = 2 * group + half
            deep = mul(m4[...], coarse_ref[half])
            here = deep[48:96]
            back = jnp.concatenate([deep[96:, :128], deep[:48, 128:]], axis=1)
            forth = jnp.concatenate([deep[:48, :128], deep[96:, 128:]], axis=1)
            if carry is None:
                carry = here + jnp.where(me == 0, 0.0, swap(back)), forth
            else:
                closing, opening = carry
                emit(step - 1, closing + joined(step, back))
                carry = here + joined(step, opening), forth
        return carry

    arrive(0)
    stage1(0)
    arrive(1)
    stage2()
    stage1(1)
    arrive(2)
    stage3()
    stage2()
    stage1(2)
    arrive(3)
    carry = stage4(0, None)
    stage3()
    stage2()
    stage1(3)

    def step(turn, carry):
        for more in range(2):
            arrive(4 + 2 * turn + more)
        for more in range(2):
            carry = stage4(1 + 2 * turn + more, carry)
            stage3()
            stage2()
            stage1(4 + 2 * turn + more)
        return carry

    carry = lax.fori_loop(0, (groups - 4) // 2, step, carry)
    carry = stage4(groups - 3, carry)
    stage3()
    stage2()
    carry = stage4(groups - 2, carry)
    stage3()
    closing, opening = stage4(groups - 1, carry)
    emit(HALF - 1, closing + jnp.where(me == HALF, 0.0, swap(opening)))


def encoder_kernel(*refs):
    volume_hbm, fetched_hbm, out_hbm = refs[0], refs[1:19], refs[19]
    volume_ref, fetched = refs[20], refs[21:39]
    laid, held = refs[39:44], refs[44:47]
    tiles, got_ref, out_ref = refs[47:50]
    fetch_sem, edge_sem, send_sem, out_sem, recv_sem = refs[50:]
    vol, me = lax.axis_index("vol"), lax.axis_index("zs")
    vols, members = lax.axis_size("vol"), lax.axis_size("zs")
    has_before, has_after = vol > 0, vol < vols - 1
    at_first, at_last = me == 0, me == members - 1

    load = pltpu.make_async_copy(volume_hbm, volume_ref, fetch_sem.at[18])
    load.start()
    loads = [
        pltpu.make_async_copy(source, target, fetch_sem.at[at])
        for at, (source, target) in enumerate(zip(fetched_hbm, fetched))
    ]
    barrier = pltpu.get_barrier_semaphore()

    def signal(vol_index, member):
        pl.semaphore_signal(barrier, inc=1, device_id=(vol_index, member), device_id_type=MESH)

    def greet(step, carry):
        signal(vol, lax.rem(me + step, members))
        return carry

    def greet_before(member, carry):
        signal(vol - 1, member)
        return carry

    def greet_after(member, carry):
        signal(vol + 1, member)
        return carry

    lax.fori_loop(1, members, greet, 0, unroll=9)

    @pl.when(has_before & at_first)
    def _():
        lax.fori_loop(0, members, greet_before, 0, unroll=8)

    @pl.when(has_after & at_last)
    def _():
        lax.fori_loop(0, members, greet_after, 0, unroll=8)

    for each in loads:
        each.start()
    load.wait()

    line = lax.broadcasted_iota(jnp.int32, (256, 256), 0)
    lane = lax.broadcasted_iota(jnp.int32, (256, 256), 1)
    parted = (line == jnp.where(lane < 128, 2 * lane, 2 * lane - 255)).astype(F32).astype(BF16)
    split = mul(volume_ref[0], parted)
    even = split[:, :128].reshape(32, 8, 128)
    odd = split[:, 128:].reshape(32, 8, 128)
    row = lax.broadcasted_iota(jnp.int32, (32, 8, 128), 1)
    upper = jnp.where(row < 4, even, pltpu.roll(odd, 4, 1))
    lower = jnp.where(row < 4, pltpu.roll(even, 4, 1), odd)
    tiles[1:65] = jnp.stack([upper, lower], axis=1).reshape(64, 8, 128).astype(BF16)

    tiles[0] = jnp.zeros((8, 128), BF16)
    tiles[65] = jnp.zeros((8, 128), BF16)

    pl.semaphore_wait(
        barrier, members - 1 + jnp.where(has_before, 1, 0) + jnp.where(has_after, 1, 0)
    )

    def give(start, count, slot, to, sem):
        return pltpu.make_async_remote_copy(
            src_ref=tiles.at[pl.ds(start, count)],
            dst_ref=got_ref.at[me, pl.ds(slot, count)],
            send_sem=sem,
            recv_sem=recv_sem.at[me],
            device_id=to,
            device_id_type=MESH,
        )

    edges = (
        (has_before & jnp.logical_not(at_first), give(1, 2, 1, (vol, 0), edge_sem.at[0])),
        (has_before, give(1, 1, 2, (vol - 1, members - 1), edge_sem.at[1])),
        (has_after & jnp.logical_not(at_last), give(63, 2, 0, (vol, members - 1), edge_sem.at[2])),
        (has_after, give(64, 1, 0, (vol + 1, 0), edge_sem.at[3])),
    )
    for wanted, copy in edges:
        pl.when(wanted)(copy.start)

    def send(step, carry):
        for target in (lax.rem(me - step + members, members), lax.rem(me + 1 + step, members)):
            partial = (has_before & (target == 0)) | (has_after & (target == members - 1))

            @pl.when(jnp.logical_not(partial) & (target != me))
            def _():
                give(target, 3, 0, (vol, target), send_sem).start()

        return carry

    lax.fori_loop(0, HALF, send, 0, unroll=4)

    def keep(start, count, slot):
        pltpu.make_async_copy(
            tiles.at[pl.ds(start, count)], got_ref.at[me, pl.ds(slot, count)], recv_sem.at[me]
        ).start()

    keep_first, keep_last = has_before & at_first, has_after & at_last
    pl.when(keep_first)(lambda: keep(1, 2, 1))
    pl.when(keep_last)(lambda: keep(63, 2, 0))
    pl.when(jnp.logical_not(keep_first | keep_last))(lambda: keep(me, 3, 0))

    for each in loads:
        each.wait()
    edge = jnp.where(
        (vol == 0) & at_first, 1, jnp.where((vol == vols - 1) & at_last, 2, 0)
    )
    lay_weights(edge, fetched[:8], fetched[8:], laid)

    def arrive(turn):
        for half in range(2):
            step = 2 * turn + half
            for z in (lax.rem(me + step, members), lax.rem(me - 1 - step + 2 * members, members)):
                pltpu.make_async_copy(got_ref.at[z], got_ref.at[z], recv_sem.at[z]).wait()

    def leave(slot):
        pltpu.make_async_copy(out_ref.at[slot], out_hbm.at[slot], out_sem).start()

    convolve_slices(me, arrive, leave, got_ref, laid, held, out_ref)

    for wanted, copy in edges:
        pl.when(wanted)(copy.wait_send)
    partials = jnp.where(edges[0][0], 1, 0) + jnp.where(edges[2][0], 1, 0)
    for count in range(3):
        @pl.when(partials == count)
        def _():
            rest = got_ref.at[pl.ds(0, 63 - count)]
            pltpu.make_async_copy(rest, rest, send_sem).wait()
    pltpu.make_async_copy(out_ref, out_hbm, out_sem).wait()


def encode(volume, *raw):
    fetched = (*raw, *tables())
    return pl.pallas_call(
        encoder_kernel,
        out_shape=jax.ShapeDtypeStruct((DEPTH, 48, 128), BF16),
        in_specs=[pl.BlockSpec(memory_space=pltpu.HBM)] * 19,
        out_specs=pl.BlockSpec(memory_space=pltpu.HBM),
        scratch_shapes=[
            pltpu.VMEM(volume.shape, BF16),
            *[pltpu.VMEM(value.shape, value.dtype) for value in fetched],
            pltpu.VMEM((256, 80), BF16),
            pltpu.VMEM((192, 512), BF16),
            pltpu.VMEM((96, 192), BF16),
            pltpu.VMEM((96, 128), F32),
            pltpu.VMEM((144, 304), BF16),
            pltpu.VMEM((2, 512, 256), BF16),
            pltpu.VMEM((2, 192, 256), BF16),
            pltpu.VMEM((2, 304, 256), BF16),
            pltpu.VMEM((66, 8, 128), BF16),
            pltpu.VMEM((DEPTH, 3, 8, 128), BF16),
            pltpu.VMEM((DEPTH, 48, 128), BF16),
            pltpu.SemaphoreType.DMA((19,)),
            pltpu.SemaphoreType.DMA((4,)),
            pltpu.SemaphoreType.DMA,
            pltpu.SemaphoreType.DMA,
            pltpu.SemaphoreType.DMA((DEPTH,)),
        ],
        compiler_params=pltpu.CompilerParams(
            collective_id=0, has_side_effects=True, vmem_limit_bytes=56 * 1024 * 1024
        ),
        name="encode",
    )(volume, *fetched)


CHUNKS = 8


def hand_kernel(source, target, held, in_sem, out_sem):
    rows = DEPTH // CHUNKS
    parts = [pl.ds(at * rows, rows) for at in range(CHUNKS)]
    into = [
        pltpu.make_async_copy(source.at[part], held.at[part], in_sem.at[at])
        for at, part in enumerate(parts)
    ]
    out = [
        pltpu.make_async_copy(held.at[part], target.at[part], out_sem.at[at])
        for at, part in enumerate(parts)
    ]
    for copy in into:
        copy.start()
    for first, second in zip(into, out):
        first.wait()
        second.start()
    for copy in out:
        copy.wait()


def hand(done):
    return pl.pallas_call(
        hand_kernel,
        out_shape=jax.ShapeDtypeStruct(done.shape, BF16),
        in_specs=[pl.BlockSpec(memory_space=pltpu.HBM)],
        out_specs=pl.BlockSpec(memory_space=pltpu.HBM),
        scratch_shapes=[
            pltpu.VMEM(done.shape, BF16),
            pltpu.SemaphoreType.DMA((CHUNKS,)),
            pltpu.SemaphoreType.DMA((CHUNKS,)),
        ],
        compiler_params=pltpu.CompilerParams(vmem_limit_bytes=56 * 1024 * 1024),
        name="hand",
    )(done)


def shards(volume, w1, o1, w2, o2, w3, o3, w4, o4):
    done = encode(
        volume,
        w1,
        o1[None],
        w2,
        o2[None],
        w3.transpose(1, 0, 2),
        o3[None],
        w4.transpose(1, 2, 0),
        o4[None],
    )
    return hand(done).reshape(DEPTH, 24, 2, 128)


def solution(mesh):
    return jax.shard_map(
        shards,
        mesh=mesh,
        in_specs=(P("zs", "vol", None), P(), P(), P(), P(), P(), P(), P(), P()),
        out_specs=P(None, None, ("vol", "zs"), None),
        check_vma=False,
    )
```

time: 33.9 us -> 28.8 us (0.85)
  the two profiles are of different devices: /device:TPU:1 before, /device:TPU:24 now
where the time goes in v3:
time: 28.8 us; the launch traced here: 28.7 us
  Pallas kernels  28.7 us (100%)
    pallas_call x1, Pallas kernels, encode(): pl.pallas_call(encoder_kernel, out_shape=jax.ShapeDtypeStruct((DEPTH, 48,...  26.7 us
    pallas_call x1, Pallas kernels, hand(): pl.pallas_call(hand_kernel, out_shape=jax.ShapeDtypeStruct(done.shape, BF...  1.99 us

profile of v3, /device:TPU:24, one launch (start us, length us, event | category | flops | bytes accessed | tf_op | source)
XLA Modules:
  0.0 28.7 jit_solution(18313780397240980072)
XLA Ops:
  0.0 26.7 %encode.1.source = bf16[64,48,128]{2,1,0:T(8,128)(2,1)} custom-call(bf16[1,256,256]{2,1,0:T(8,128)(2,1)} %refs_0_.1, bf16[9,12]{1,0:T(8,128)(2,1)} %refs_1_.1, f32[1,12]{1,0:T(1,128)} %bitcast.9, bf16[9,12,12]{2,1,0:T(8,128)(2,1)} %refs_3_.1, f32[1,12]{1,0:T(1,128)} %bitcast.10, bf16[12,4,24]{2,1,0:T(4,128)(2,1)} %bitcast.8, f32[1,24]{1,0:T(1,128)} %bitcast.11, ...), custom_call_target="tpu_custom_call" | custom-call | tf_op jit(solution)/shard_map/encode/pallas_call | solution.py:424
  26.7 2.0 %hand.1 = bf16[64,48,128]{2,1,0:T(8,128)(2,1)} custom-call(bf16[64,48,128]{2,1,0:T(8,128)(2,1)} %encode.1.source), custom_call_target="tpu_custom_call" | custom-call | tf_op jit(solution)/shard_map/hand/pallas_call | solution.py:480

commit v4 on v3

--- a/solution.py
+++ b/solution.py
@@ -164,7 +164,7 @@
     return jnp.concatenate([value[:, 128:], value[:, :128]], axis=1)
 
 
-def place_first(x_ref, m1, first_ref, lows):
+def place_first(x_ref, m1, first_ref, lows, spot):
     for half, (low, high) in enumerate(lows):
         field = jnp.concatenate(
             [x_ref[low].astype(F32).reshape(24, 128), x_ref[high].astype(F32).reshape(24, 128)], axis=1
@@ -181,29 +181,29 @@
         stacked = jnp.concatenate([before, field, after, jnp.ones((8, 256), F32)], axis=0)
         first = relu(mul(m1[...], stacked.astype(BF16)))
         even, odd = first[:128], first[128:]
-        first_ref[half, :128] = both(from_left, odd)
-        first_ref[half, 128:256] = even
-        first_ref[half, 256:384] = odd
-        first_ref[half, 384:] = both(from_right, even)
-
-
-def place_second(first_ref, m2, second_ref):
-    for half in range(2):
-        second_ref[half] = relu(mul(m2[...], first_ref[half]))
-
-
-def place_coarse(second_ref, m3, b3, coarse_ref):
-    for half in range(2):
-        coarse = relu(mul(m3[...], second_ref[half]) + twice(b3[...]))
-        coarse_ref[half, :96] = both(from_left, coarse)
-        coarse_ref[half, 96:192] = coarse
-        coarse_ref[half, 192:288] = both(from_right, coarse)
+        first_ref[spot + half, :128] = both(from_left, odd)
+        first_ref[spot + half, 128:256] = even
+        first_ref[spot + half, 256:384] = odd
+        first_ref[spot + half, 384:] = both(from_right, even)
+
+
+def place_second(first_ref, m2, second_ref, spot):
+    for at in (spot, spot + 1):
+        second_ref[at] = relu(mul(m2[...], first_ref[at]))
+
+
+def place_coarse(second_ref, m3, b3, coarse_ref, spot):
+    for at in (spot, spot + 1):
+        coarse = relu(mul(m3[...], second_ref[at]) + twice(b3[...]))
+        coarse_ref[at, :96] = both(from_left, coarse)
+        coarse_ref[at, 96:192] = coarse
+        coarse_ref[at, 192:288] = both(from_right, coarse)
 
 
 def convolve_slices(me, arrive, leave, x_ref, laid, held, out_ref):
     m1, m2, m3, b3, m4 = laid
     first_ref, second_ref, coarse_ref = held
-    coarse_ref[:, 288:] = jnp.ones((2, 16, 256), BF16)
+    coarse_ref[:, 288:] = jnp.ones((4, 16, 256), BF16)
     groups = HALF // 2
 
     def up(step):
@@ -212,15 +212,15 @@
     def down(step):
         return lax.rem(me - 1 - step + 2 * DEPTH, DEPTH)
 
-    def stage1(turn):
+    def stage1(turn, odd):
         pairs = [(up(2 * turn + half), down(2 * turn + half)) for half in range(2)]
-        place_first(x_ref, m1, first_ref, pairs)
-
-    def stage2():
-        place_second(first_ref, m2, second_ref)
-
-    def stage3():
-        place_coarse(second_ref, m3, b3, coarse_ref)
+        place_first(x_ref, m1, first_ref, pairs, 2 * odd)
+
+    def stage2(odd):
+        place_second(first_ref, m2, second_ref, 2 * odd)
+
+    def stage3(odd):
+        place_coarse(second_ref, m3, b3, coarse_ref, 2 * odd)
 
     def joined(step, part):
         low = jnp.where(up(step) == 0, 0.0, part[:, :128])
@@ -233,10 +233,10 @@
         leave(up(step))
         leave(down(step))
 
-    def stage4(group, carry):
+    def stage4(group, odd, carry):
         for half in range(2):
             step = 2 * group + half
-            deep = mul(m4[...], coarse_ref[half])
+            deep = mul(m4[...], coarse_ref[2 * odd + half])
             here = deep[48:96]
             back = jnp.concatenate([deep[96:, :128], deep[:48, 128:]], axis=1)
             forth = jnp.concatenate([deep[:48, :128], deep[96:, 128:]], axis=1)
@@ -249,37 +249,47 @@
         return carry
 
     arrive(0)
-    stage1(0)
+    stage1(0, 0)
     arrive(1)
-    stage2()
-    stage1(1)
+    stage2(0)
+    stage1(1, 1)
     arrive(2)
-    stage3()
-    stage2()
-    stage1(2)
+    stage3(0)
+    stage2(1)
+    stage1(2, 0)
     arrive(3)
-    carry = stage4(0, None)
-    stage3()
-    stage2()
-    stage1(3)
+    carry = stage4(0, 0, None)
+    stage3(1)
+    stage2(0)
+    stage1(3, 1)
 
     def step(turn, carry):
         for more in range(2):
             arrive(4 + 2 * turn + more)
         for more in range(2):
-            carry = stage4(1 + 2 * turn + more, carry)
-            stage3()
-            stage2()
-            stage1(4 + 2 * turn + more)
+            carry = stage4(1 + 2 * turn + more, 1 - more, carry)
+            stage3(more)
+            stage2(1 - more)
+            stage1(4 + 2 * turn + more, more)
         return carry
 
-    carry = lax.fori_loop(0, (groups - 4) // 2, step, carry)
-    carry = stage4(groups - 3, carry)
-    stage3()
-    stage2()
-    carry = stage4(groups - 2, carry)
-    stage3()
-    closing, opening = stage4(groups - 1, carry)
+    carry = lax.fori_loop(0, (groups - 6) // 2, step, carry)
+    arrive(groups - 2)
+    carry = stage4(groups - 5, 1, carry)
+    stage3(0)
+    stage2(1)
+    stage1(groups - 2, 0)
+    arrive(groups - 1)
+    stage1(groups - 1, 1)
+    carry = stage4(groups - 4, 0, carry)
+    stage2(0)
+    stage3(1)
+    stage2(1)
+    stage3(0)
+    carry = stage4(groups - 3, 1, carry)
+    stage3(1)
+    carry = stage4(groups - 2, 0, carry)
+    closing, opening = stage4(groups - 1, 1, carry)
     emit(HALF - 1, closing + jnp.where(me == HALF, 0.0, swap(opening)))
 
 
@@ -378,7 +388,7 @@
 
         return carry
 
-    lax.fori_loop(0, HALF, send, 0, unroll=4)
+    lax.fori_loop(0, 8, send, 0, unroll=4)
 
     def keep(start, count, slot):
         pltpu.make_async_copy(
@@ -396,8 +406,11 @@
         (vol == 0) & at_first, 1, jnp.where((vol == vols - 1) & at_last, 2, 0)
     )
     lay_weights(edge, fetched[:8], fetched[8:], laid)
+    lax.fori_loop(8, 16, send, 0, unroll=4)
 
     def arrive(turn):
+        if isinstance(turn, int) and 16 + 4 * turn < HALF:
+            lax.fori_loop(16 + 4 * turn, 16 + 4 * (turn + 1), send, 0, unroll=4)
         for half in range(2):
             step = 2 * turn + half
             for z in (lax.rem(me + step, members), lax.rem(me - 1 - step + 2 * members, members)):
@@ -434,9 +447,9 @@
             pltpu.VMEM((96, 192), BF16),
             pltpu.VMEM((96, 128), F32),
             pltpu.VMEM((144, 304), BF16),
-            pltpu.VMEM((2, 512, 256), BF16),
-            pltpu.VMEM((2, 192, 256), BF16),
-            pltpu.VMEM((2, 304, 256), BF16),
+            pltpu.VMEM((4, 512, 256), BF16),
+            pltpu.VMEM((4, 192, 256), BF16),
+            pltpu.VMEM((4, 304, 256), BF16),
             pltpu.VMEM((66, 8, 128), BF16),
             pltpu.VMEM((DEPTH, 3, 8, 128), BF16),
             pltpu.VMEM((DEPTH, 48, 128), BF16),
@@ -453,7 +466,7 @@
     )(volume, *fetched)
 
 
-CHUNKS = 8
+CHUNKS = 4
 
 
 def hand_kernel(source, target, held, in_sem, out_sem):

time: 28.8 us -> 28.5 us (0.990)
  the two profiles are of different devices: /device:TPU:24 before, /device:TPU:22 now
where the time goes in v4:
time: 28.5 us; the launch traced here: 28.3 us
  Pallas kernels  28.3 us (99%)
    pallas_call x1, Pallas kernels, encode(): pl.pallas_call(encoder_kernel, out_shape=jax.ShapeDtypeStruct((DEPTH, 48,...  26.3 us
    pallas_call x1, Pallas kernels, hand(): pl.pallas_call(hand_kernel, out_shape=jax.ShapeDtypeStruct(done.shape, BF...  1.96 us

profile of v4, /device:TPU:22, one launch (start us, length us, event | category | flops | bytes accessed | tf_op | source)
XLA Modules:
  0.0 28.3 jit_solution(13118153720540573863)
XLA Ops:
  0.0 26.3 %encode.1.source = bf16[64,48,128]{2,1,0:T(8,128)(2,1)} custom-call(bf16[1,256,256]{2,1,0:T(8,128)(2,1)} %refs_0_.1, bf16[9,12]{1,0:T(8,128)(2,1)} %refs_1_.1, f32[1,12]{1,0:T(1,128)} %bitcast.9, bf16[9,12,12]{2,1,0:T(8,128)(2,1)} %refs_3_.1, f32[1,12]{1,0:T(1,128)} %bitcast.10, bf16[12,4,24]{2,1,0:T(4,128)(2,1)} %bitcast.8, f32[1,24]{1,0:T(1,128)} %bitcast.11, ...), custom_call_target="tpu_custom_call" | custom-call | tf_op jit(solution)/shard_map/encode/pallas_call | solution.py:437
  26.4 2.0 %hand.1 = bf16[64,48,128]{2,1,0:T(8,128)(2,1)} custom-call(bf16[64,48,128]{2,1,0:T(8,128)(2,1)} %encode.1.source), custom_call_target="tpu_custom_call" | custom-call | tf_op jit(solution)/shard_map/hand/pallas_call | solution.py:493

commit v5 on v4

--- a/solution.py
+++ b/solution.py
@@ -315,8 +315,8 @@
     def signal(vol_index, member):
         pl.semaphore_signal(barrier, inc=1, device_id=(vol_index, member), device_id_type=MESH)
 
-    def greet(step, carry):
-        signal(vol, lax.rem(me + step, members))
+    def greet(member, carry):
+        pl.when(member != me)(lambda: signal(vol, member))
         return carry
 
     def greet_before(member, carry):
@@ -327,7 +327,7 @@
         signal(vol + 1, member)
         return carry
 
-    lax.fori_loop(1, members, greet, 0, unroll=9)
+    lax.fori_loop(0, members, greet, 0, unroll=8)
 
     @pl.when(has_before & at_first)
     def _():

time: 28.5 us -> 28.4 us (level)
  the two profiles are of different devices: /device:TPU:22 before, /device:TPU:1 now
where the time goes in v5:
time: 28.4 us; the launch traced here: 27.9 us
  Pallas kernels  27.9 us (98%)
    pallas_call x1, Pallas kernels, encode(): pl.pallas_call(encoder_kernel, out_shape=jax.ShapeDtypeStruct((DEPTH, 48,...  25.9 us
    pallas_call x1, Pallas kernels, hand(): pl.pallas_call(hand_kernel, out_shape=jax.ShapeDtypeStruct(done.shape, BF...  1.96 us

profile of v5, /device:TPU:1, one launch (start us, length us, event | category | flops | bytes accessed | tf_op | source)
XLA Modules:
  0.0 27.9 jit_solution(4693103755697512410)
XLA Ops:
  0.0 25.9 %encode.1.source = bf16[64,48,128]{2,1,0:T(8,128)(2,1)} custom-call(bf16[1,256,256]{2,1,0:T(8,128)(2,1)} %refs_0_.1, bf16[9,12]{1,0:T(8,128)(2,1)} %refs_1_.1, f32[1,12]{1,0:T(1,128)} %bitcast.9, bf16[9,12,12]{2,1,0:T(8,128)(2,1)} %refs_3_.1, f32[1,12]{1,0:T(1,128)} %bitcast.10, bf16[12,4,24]{2,1,0:T(4,128)(2,1)} %bitcast.8, f32[1,24]{1,0:T(1,128)} %bitcast.11, ...), custom_call_target="tpu_custom_call" | custom-call | tf_op jit(solution)/shard_map/encode/pallas_call | solution.py:437
  25.9 2.0 %hand.1 = bf16[64,48,128]{2,1,0:T(8,128)(2,1)} custom-call(bf16[64,48,128]{2,1,0:T(8,128)(2,1)} %encode.1.source), custom_call_target="tpu_custom_call" | custom-call | tf_op jit(solution)/shard_map/hand/pallas_call | solution.py:493

commit v6 on v5

--- a/solution.py
+++ b/solution.py
@@ -267,10 +267,10 @@
         for more in range(2):
             arrive(4 + 2 * turn + more)
         for more in range(2):
+            stage1(4 + 2 * turn + more, more)
+            stage2(1 - more)
+            stage3(more)
             carry = stage4(1 + 2 * turn + more, 1 - more, carry)
-            stage3(more)
-            stage2(1 - more)
-            stage1(4 + 2 * turn + more, more)
         return carry
 
     carry = lax.fori_loop(0, (groups - 6) // 2, step, carry)

time: 28.4 us -> 28.3 us (level)
  the two profiles are of different devices: /device:TPU:1 before, /device:TPU:8 now
where the time goes in v6:
time: 28.3 us; the launch traced here: 28.2 us
  Pallas kernels  28.2 us (100%)
    pallas_call x1, Pallas kernels, encode(): pl.pallas_call(encoder_kernel, out_shape=jax.ShapeDtypeStruct((DEPTH, 48,...  26.2 us
    pallas_call x1, Pallas kernels, hand(): pl.pallas_call(hand_kernel, out_shape=jax.ShapeDtypeStruct(done.shape, BF...  1.96 us

profile of v6, /device:TPU:8, one launch (start us, length us, event | category | flops | bytes accessed | tf_op | source)
XLA Modules:
  0.0 28.2 jit_solution(12357068022777389409)
XLA Ops:
  0.0 26.2 %encode.1.source = bf16[64,48,128]{2,1,0:T(8,128)(2,1)} custom-call(bf16[1,256,256]{2,1,0:T(8,128)(2,1)} %refs_0_.1, bf16[9,12]{1,0:T(8,128)(2,1)} %refs_1_.1, f32[1,12]{1,0:T(1,128)} %bitcast.9, bf16[9,12,12]{2,1,0:T(8,128)(2,1)} %refs_3_.1, f32[1,12]{1,0:T(1,128)} %bitcast.10, bf16[12,4,24]{2,1,0:T(4,128)(2,1)} %bitcast.8, f32[1,24]{1,0:T(1,128)} %bitcast.11, ...), custom_call_target="tpu_custom_call" | custom-call | tf_op jit(solution)/shard_map/encode/pallas_call | solution.py:437
  26.2 2.0 %hand.1 = bf16[64,48,128]{2,1,0:T(8,128)(2,1)} custom-call(bf16[64,48,128]{2,1,0:T(8,128)(2,1)} %encode.1.source), custom_call_target="tpu_custom_call" | custom-call | tf_op jit(solution)/shard_map/hand/pallas_call | solution.py:493
